TPU v7x, 256 devices: a whole 4x4x8 slice. The times are simulated.
256 devices in a mesh: pos: 32 (over x, z), ch: 8 (over y, core).
Axes of the slice: x: 4, y: 4, z: 8, core: 2. Of those that a mesh axis runs over, the one named last changes fastest.
Arguments:
- track_grad: bfloat16 [768, 262144], P('ch', 'pos'), may hold values from -6 to 6
- activation: bfloat16 [768, 262144], P('ch', 'pos'), may hold values from -6 to 6
- coarse_in: bfloat16 [768, 131072], P('ch', 'pos'), may hold values from -6 to 6
- tap_weight: bfloat16 [4, 768, 768], P(None, 'ch'), may hold values from -0.15625 to 0.15625
- score_grad: float32 [65536], P('pos'), may hold values from -96 to 96
- donor_row: int32 [65536], P('pos'), may hold values from 0 to 8191
- acceptor_owner: int32 [65536, 1], P('pos'), may hold values from 0 to 31; in each aligned block of 2048 rows (0 to 2047, 2048 to 4095, ...) at most 256 rows name the same one
- acceptor_row: int32 [65536], P('pos'), may hold values from 0 to 8191
Outputs:
- skip_grad: bfloat16 [768, 262144], P('ch', 'pos')
- coarse_grad: bfloat16 [768, 131072], P('ch', 'pos')
- weight_grad: bfloat16 [4, 768, 768], P(None, 'ch', 'pos')
Inputs may be any that keep to these rules, and one draw needn't show every extreme that they name: `acceptor_owner`: within the 2048 rows of one index of pos, no value appears more than 256 times; some value appears exactly 256 times.
All inputs are finite; a program needn't handle non-finite values.
Results may differ from a plain program's by a relative error of at most 0.0043.
Values may be sent and summed in bfloat16 or wider, within the bound.
A program may use at most 128 MiB of HBM per device.

v0:
```python
import math

import jax
import jax.numpy as jnp
from jax import lax
from jax.sharding import PartitionSpec as P

C = 768
KERNEL = 4


def extended_2(x, sides, width):
    for axis, dim in sides:
        devices, length = (lax.axis_size(axis), x.shape[dim])
        up = [(i, (i + 1) % devices) for i in range(devices - 1)]
        down = [(j, i) for i, j in up]
        last = lax.slice_in_dim(x, length - width, length, axis=dim)
        initial = lax.slice_in_dim(x, 0, width, axis=dim)
        before = lax.ppermute(last, axis, up)
        after = lax.ppermute(initial, axis, down)
        x = jnp.concatenate([before, x, after], axis=dim)
    return x


def shards(
    track_grad,
    activation,
    coarse_in,
    tap_weight,
    score_grad,
    donor_row,
    acceptor_owner,
    acceptor_row,
):
    chan_local, local_len = track_grad.shape
    junc_count = score_grad.shape[0]
    pos_count = lax.axis_size("pos")
    capacity = junc_count // 8
    factor = score_grad * (1.0 / math.sqrt(C))
    owners = acceptor_owner[:, 0]
    members = (owners[:, None] == jnp.arange(pos_count, dtype=jnp.int32)[None, :]).astype(jnp.int32)
    rank_list = jnp.cumsum(members, axis=0) - 1
    within = jnp.sum(rank_list * members, axis=1)
    flat_slot = owners * capacity + within
    request_rows = (
        jnp.zeros((pos_count * capacity,), jnp.int32)
        .at[flat_slot]
        .set(acceptor_row)
        .reshape(1, pos_count, capacity)
    )
    donor_vals = jnp.take(activation, donor_row, axis=1).astype(jnp.float32)
    acceptor_terms = (donor_vals * factor[None, :]).astype(jnp.bfloat16)
    term_buffer = (
        jnp.zeros((chan_local, pos_count * capacity), jnp.bfloat16)
        .at[:, flat_slot]
        .set(acceptor_terms)
        .reshape(chan_local, pos_count, capacity)
    )
    got_rows = lax.all_to_all(request_rows, "pos", split_axis=1, concat_axis=1, tiled=True)
    fetched = jnp.take(activation, got_rows[0], axis=1)
    returned = lax.all_to_all(fetched, "pos", split_axis=1, concat_axis=1, tiled=True)
    got_terms = lax.all_to_all(term_buffer, "pos", split_axis=1, concat_axis=1, tiled=True)
    acceptor_vals = returned[:, owners, within].astype(jnp.float32)
    running = track_grad.astype(jnp.float32)
    running = running.at[:, donor_row].add(acceptor_vals * factor[None, :])
    running = running.at[:, got_rows.reshape(-1)].add(
        got_terms.reshape(chan_local, -1).astype(jnp.float32)
    )
    skip_grad = running.astype(jnp.bfloat16)
    extended = extended_2(skip_grad, (("pos", 1),), 1)
    tap_stack = jnp.stack(
        [extended[:, offset : offset + local_len : 2] for offset in range(KERNEL)]
    )
    full_in = lax.all_gather(coarse_in, "ch", axis=0, tiled=True)
    summed = lax.psum_scatter(
        jnp.einsum("ip,kop->iko", full_in, tap_stack, preferred_element_type=jnp.float32),
        "pos",
        scatter_dimension=0,
        tiled=True,
    )
    coarse_total = coarse_in.shape[1] * pos_count
    weight_grad = (summed.transpose(1, 2, 0) * (1.0 / math.sqrt(coarse_total))).astype(jnp.bfloat16)
    coarse_grad = lax.psum_scatter(
        jnp.einsum("koi,kop->ip", tap_weight, tap_stack, preferred_element_type=jnp.float32),
        "ch",
        scatter_dimension=0,
        tiled=True,
    ).astype(jnp.bfloat16)
    return (skip_grad, coarse_grad, weight_grad)


def solution(mesh):
    in_specs = (
        P("ch", "pos"),
        P("ch", "pos"),
        P("ch", "pos"),
        P(None, "ch", None),
        P("pos"),
        P("pos"),
        P("pos", None),
        P("pos"),
    )
    out_specs = (P("ch", "pos"), P("ch", "pos"), P(None, "ch", "pos"))
    return jax.shard_map(shards, mesh=mesh, in_specs=in_specs, out_specs=out_specs, check_vma=False)
```

profile of v0, /device:TPU:1, one launch (start us, length us, event | category | flops | bytes accessed | tf_op | source)
XLA Modules:
  0.0 609.1 jit_solution(7359044255455288285)
XLA Ops:
  7.2 0.0 copy-start
  7.2 0.0 copy-start.3
  7.2 0.0 copy-start.5
  7.2 0.0 copy-start.4
  7.2 0.0 all-gather.2.cloned.1.call-start
  7.3 0.7 all-gather.2.cloned.1.call-update
  7.9 0.7 fusion.17
  8.7 9.1 %reduce-window.6 = s32[32,16,128]{2,1,0:T(8,128)S(1)} reduce-window(s32[32,16,128]{2,1,0:T(8,128)S(1)} %fusion.17, s32[]{:T(128)} %constant.17.clone.1), window={size=1x1x128 pad=0_0x0_0x127_0}, to_apply=%region_0.0 | reduce-window | flops 8323072 | bytes 524292 | tf_op jit(solution)/shard_map/reduce-window
  17.7 0.1 slice.38
  17.9 0.2 copy.65
  18.1 0.2 reduce-window.9
  18.3 0.1 add_add_fusion
  18.5 0.8 fusion.15
  19.3 0.0 copy-done.3
  19.3 0.1 fusion.24
  19.3 8.8 %scatter_custom_fusion = s32[8192]{0:T(1024)} fusion(s32[2048]{0:T(1024)S(1)} %bitcast.83, s32[2048]{0:T(1024)} %param.15, s32[]{:T(128)} %constant.17.clone.1), kind=kCustom, calls=%fused_computation.44 | custom fusion | bytes 33280 | tf_op jit(solution)/shard_map/scatter | solution.py:48
  28.1 11.9 %all-to-all-start = ((s32[1,32,256]{2,0,1:T(1,128)}), s32[1,32,256]{2,0,1:T(1,128)S(1)}, u32[]{:S(2)}, u32[]{:S(2)}) async-start(s32[1,32,256]{2,0,1:T(1,128)} %bitcast.7), calls=%async_computation | async-start | bytes 65536 | tf_op jit(solution)/shard_map/all_to_all | solution.py:59
  40.0 0.0 copy-done.5
  40.1 3.1 copy.53
  43.2 15.0 %scatter_custom_fusion.2 = bf16[96,8192]{0,1:T(8,128)(2,1)} fusion(s32[2048]{0:T(1024)S(1)} %bitcast.84, bf16[]{:T(256)} %constant.48.clone.1, f32[2048]{0:T(1024)S(1)} %broadcast_multiply_fusion, pred[2048]{0:T(1024)(128)(4,1)S(1)} %compare_and_fusion.1, bf16[]{:T(256)} %constant.28.clone.1, bf16[96,8192]{0,1:T(8,128)(2,1)S(1)} %copy.53, ...), kind=kCustom, calls=%fused_computation.18 | custom fusion | flops 786432 | bytes 3688452 | tf_op jit(solution)/shard_map/scatter | solution.py:56
  58.2 3.9 copy.58
  62.1 0.0 all-to-all-done
  62.1 9.3 %all-to-all-start.2 = ((bf16[96,32,256]{2,0,1:T(8,128)(2,1)}), bf16[96,32,256]{2,0,1:T(8,128)(2,1)}, u32[]{:S(2)}, u32[]{:S(2)}) async-start(bf16[96,32,256]{2,0,1:T(8,128)(2,1)} %copy.58), calls=%async_computation.2 | async-start | bytes 3145728 | tf_op jit(solution)/shard_map/all_to_all | solution.py:62
  71.6 29.4 %gather_fusion = bf16[8192,96]{1,0:T(8,128)(2,1)} fusion(bf16[96,8192]{0,1:T(8,128)(2,1)S(1)} %copy.53, s32[8192]{0:T(1024)S(1)} %broadcast_clamp_fusion), kind=kCustom, calls=%fused_computation | custom fusion | bytes 3178496 | tf_op jit(solution)/shard_map/jit(_take)/gather | solution.py:60
  101.0 3.1 copy.54
  104.1 1.3 select_bitcast_fusion
  105.4 2.9 all-to-all-done.2
  108.3 7.8 %all-to-all-start.1 = ((bf16[96,32,256]{2,0,1:T(8,128)(2,1)}), bf16[96,32,256]{2,0,1:T(8,128)(2,1)}, u32[]{:S(2)}, u32[]{:S(2)}) async-start(bf16[96,32,256]{2,0,1:T(8,128)(2,1)} %select_bitcast_fusion), calls=%async_computation.1 | async-start | bytes 3145728 | tf_op jit(solution)/shard_map/all_to_all | solution.py:61
  116.1 0.2 all-reduce.3.cloned.1.call-start
  116.3 2.9 copy.56
  119.2 1.8 convert_bitcast_fusion
  121.0 2.0 copy.69
  122.9 5.1 copy.60
  128.1 24.8 %all-to-all-done.1 = bf16[96,32,256]{2,0,1:T(8,128)(2,1)} async-done(((bf16[96,32,256]{2,0,1:T(8,128)(2,1)}), bf16[96,32,256]{2,0,1:T(8,128)(2,1)}, u32[]{:S(2)}, u32[]{:S(2)}) %all-to-all-start.1) | async-done | bytes 1572896 | tf_op jit(solution)/shard_map/all_to_all | solution.py:61
  152.9 3.1 copy.55
  156.0 25.5 %scatter_custom_fusion.1 = f32[96,8192]{0,1:T(8,128)} fusion(f32[96,8192]{0,1:T(8,128)} %copy.56, s32[2048]{0:T(1024)S(1)} %get-tuple-element.23, f32[2048]{0:T(1024)S(1)} %broadcast_multiply_fusion, bf16[96,32,256]{0,2,1:T(8,128)(2,1)S(1)} %copy.55, s32[2048]{0:T(1024)S(1)} %bitcast.81), kind=kCustom, calls=%fused_computation.15 | custom fusion | flops 589824 | bytes 5259264 | tf_op jit(solution)/shard_map/scatter-add | solution.py:65
  181.4 59.1 %scatter_fusion = f32[96,8192]{0,1:T(8,128)} fusion(f32[96,8192]{0,1:T(8,128)} %scatter_custom_fusion.1, s32[8192]{0:T(1024)S(1)} %bitcast.76, f32[8192,96]{1,0:T(8,128)} %copy.60), kind=kCustom, calls=%fused_computation.6 | custom fusion | flops 786432 | bytes 9469952 | tf_op jit(solution)/shard_map/scatter-add | solution.py:66
  240.5 3.4 copy.61
  243.9 0.0 copy-start.1
  243.9 0.1 fusion.31
  244.0 1.3 collective-permute-start.1
  245.3 4.2 collective-permute-start
  249.5 26.9 %slice.29 = bf16[96,4096]{1,0:T(8,128)(2,1)S(1)} slice(bf16[96,8192]{1,0:T(8,128)(2,1)S(1)} %copy.61), slice={[0:96:1], [0:8192:2]} | slice | bytes 1572864 | tf_op jit(solution)/shard_map/slice | solution.py:72
  276.4 0.0 collective-permute-done.1
  276.4 0.0 collective-permute-done
  276.4 2.7 concatenate.7
  279.2 28.4 %slice.31 = bf16[96,4096]{1,0:T(8,128)(2,1)} slice(bf16[96,8194]{1,0:T(8,128)(2,1)} %concatenate.7), slice={[0:96:1], [3:8194:2]} | slice | bytes 1572864 | tf_op jit(solution)/shard_map/slice | solution.py:72
  307.5 28.4 %slice.30 = bf16[96,4096]{1,0:T(8,128)(2,1)} slice(bf16[96,8194]{1,0:T(8,128)(2,1)} %concatenate.7), slice={[0:96:1], [2:8194:2]} | slice | bytes 1572864 | tf_op jit(solution)/shard_map/slice | solution.py:72
  335.9 28.4 %slice.28 = bf16[96,4096]{1,0:T(8,128)(2,1)} slice(bf16[96,8194]{1,0:T(8,128)(2,1)} %concatenate.7), slice={[0:96:1], [0:8192:2]} | slice | bytes 1572864 | tf_op jit(solution)/shard_map/slice | solution.py:72
  364.3 6.2 %fusion.2 = f32[768,4,96]{0,2,1:T(8,128)S(1)} fusion(bf16[768,4096]{1,0:T(8,128)(2,1)} %all-gather.2.cloned.1.call-done, bf16[1,96,4096]{2,1,0:T(8,128)(2,1)} %bitcast.68, bf16[1,96,4096]{2,1,0:T(8,128)(2,1)} %bitcast.70, bf16[1,96,4096]{2,1,0:T(8,128)(2,1)S(1)} %bitcast.66, bf16[1,96,4096]{2,1,0:T(8,128)(2,1)} %bitcast.72), kind=kOutput, calls=%fused_computation.13 | convolution fusion | flops 2420637696 | bytes 10616832 | tf_op jit(solution)/shard_map/ip,kop->iko/dot_general | solution.py:76
  370.5 1.5 copy.62
  372.0 0.0 all-reduce.3.cloned.1.call-update
  372.0 0.3 reduce-scatter.4.cloned.1.call-start
  372.3 9.6 %convolution_bitcast_fusion = f32[768,4096]{0,1:T(8,128)} fusion(bf16[4,96,768]{2,1,0:T(8,128)(2,1)S(1)} %copy-done, bf16[1,96,4096]{2,1,0:T(8,128)(2,1)} %bitcast.69, bf16[1,96,4096]{2,1,0:T(8,128)(2,1)} %bitcast.71, bf16[1,96,4096]{2,1,0:T(8,128)(2,1)S(1)} %bitcast.67, bf16[1,96,4096]{2,1,0:T(8,128)(2,1)} %bitcast.73), kind=kOutput, calls=%fused_computation.7 | convolution fusion | flops 2420637696 | bytes 16318464 | tf_op jit(solution)/shard_map/koi,kop->ip/dot_general | solution.py:84
  381.9 12.8 %copy.66 = f32[768,4096]{1,0:T(8,128)} copy(f32[768,4096]{0,1:T(8,128)} %convolution_bitcast_fusion) | data formatting | bytes 25165824
  394.7 0.0 reduce-scatter.4.cloned.1.call-update
  394.7 0.6 copy-done.6
  395.3 0.6 dynamic-slice
  396.6 124.7 %all-reduce.3.cloned.1.call-done = f32[768,4,96]{2,1,0:T(4,128)} async-done(((f32[768,4,96]{2,1,0:T(4,128)}), f32[768,4,96]{2,1,0:T(4,128)}) %all-reduce.3.cloned.1.call-update) | async-done | bytes 1179664
  521.3 0.8 fusion.19
  522.1 0.6 copy.64
  522.8 76.8 %reduce-scatter.4.cloned.1.call-done = f32[96,4096]{1,0:T(8,128)} async-done(((f32[768,4096]{1,0:T(8,128)}), f32[96,4096]{1,0:T(8,128)}) %reduce-scatter.4.cloned.1.call-update) | async-done | bytes 1572880
  599.6 1.7 copy.67
  601.3 1.2 copy.63
  (14 shorter events, 0.1 us)
Async XLA Ops:
  7.2 365.2 %copy-start = (bf16[4,96,768]{2,1,0:T(8,128)(2,1)S(1)}, bf16[4,96,768]{2,1,0:T(8,128)(2,1)}, u32[]{:S(2)}) copy-start(bf16[4,96,768]{2,1,0:T(8,128)(2,1)} %param.11) | copy-start | bytes 1769476
  7.2 12.1 %copy-start.3 = (s32[2048,1]{0,1:T(1,128)S(1)}, s32[2048,1]{0,1:T(1,128)}, u32[]{:S(2)}) copy-start(s32[2048,1]{0,1:T(1,128)} %param.14) | copy-start | bytes 24580
  7.2 32.8 %copy-start.5 = (f32[2048]{0:T(1024)S(1)}, f32[2048]{0:T(1024)}, u32[]{:S(2)}) copy-start(f32[2048]{0:T(1024)} %param.12) | copy-start | bytes 24580
  7.2 32.8 %copy-start.4 = (s32[2048]{0:T(1024)S(1)}, s32[2048]{0:T(1024)}, u32[]{:S(2)}) copy-start(s32[2048]{0:T(1024)} %param.13) | copy-start | bytes 24580
  7.2 357.1 %all-gather.2.cloned.1.call-start = ((), (), s32[]{:S(2)}) async-start(), calls=%async_computation.4 | async-start | bytes 7077888 | tf_op jit(solution)/shard_map/all_gather | solution.py:74
  28.1 34.0 %all-to-all-start = ((s32[1,32,256]{2,0,1:T(1,128)}), s32[1,32,256]{2,0,1:T(1,128)S(1)}, u32[]{:S(2)}, u32[]{:S(2)}) async-start(s32[1,32,256]{2,0,1:T(1,128)} %bitcast.7), calls=%async_computation | async-start | bytes 65536 | tf_op jit(solution)/shard_map/all_to_all | solution.py:59
  62.1 46.1 %all-to-all-start.2 = ((bf16[96,32,256]{2,0,1:T(8,128)(2,1)}), bf16[96,32,256]{2,0,1:T(8,128)(2,1)}, u32[]{:S(2)}, u32[]{:S(2)}) async-start(bf16[96,32,256]{2,0,1:T(8,128)(2,1)} %copy.58), calls=%async_computation.2 | async-start | bytes 3145728 | tf_op jit(solution)/shard_map/all_to_all | solution.py:62
  105.4 10.9 %copy-start.2 = (bf16[96,8192]{1,0:T(8,128)(2,1)S(1)}, bf16[96,8192]{1,0:T(8,128)(2,1)}, u32[]{:S(2)}) copy-start(bf16[96,8192]{1,0:T(8,128)(2,1)} %param.8) | copy-start | bytes 4718596
  108.3 44.6 %all-to-all-start.1 = ((bf16[96,32,256]{2,0,1:T(8,128)(2,1)}), bf16[96,32,256]{2,0,1:T(8,128)(2,1)}, u32[]{:S(2)}, u32[]{:S(2)}) async-start(bf16[96,32,256]{2,0,1:T(8,128)(2,1)} %select_bitcast_fusion), calls=%async_computation.1 | async-start | bytes 3145728 | tf_op jit(solution)/shard_map/all_to_all | solution.py:61
  116.1 405.3 %all-reduce.3.cloned.1.call-start = ((), (), s32[]{:S(2)}) async-start(), calls=%async_computation.6 | async-start | bytes 3145728
  243.9 63.6 %copy-start.1 = (bf16[96,8192]{1,0:T(8,128)(2,1)}, bf16[96,8192]{1,0:T(8,128)(2,1)S(1)}, u32[]{:S(2)}) copy-start(bf16[96,8192]{1,0:T(8,128)(2,1)S(1)} %copy.61) | copy-start | bytes 4718596
  244.0 32.4 %collective-permute-start.1 = (bf16[96,1]{1,0:T(8,128)(2,1)S(1)}, bf16[96,1]{1,0:T(8,128)(2,1)S(1)}, u32[]{:S(2)}, u32[]{:S(2)}) collective-permute-start(bf16[96,1]{1,0:T(8,128)(2,1)S(1)} %get-tuple-element.18), channel_id=1, source_target_pairs={{8,0},{16,8},{24,16},{32,24},{40,32},{48,40},{56,48},{64,56},{72,6... | collective-permute-start | bytes 584 | tf_op jit(solution)/shard_map/ppermute | solution.py:20
  245.3 31.1 %collective-permute-start = (bf16[96,1]{1,0:T(8,128)(2,1)S(1)}, bf16[96,1]{1,0:T(8,128)(2,1)S(1)}, u32[]{:S(2)}, u32[]{:S(2)}) collective-permute-start(bf16[96,1]{1,0:T(8,128)(2,1)S(1)} %get-tuple-element.19), channel_id=1, source_target_pairs={{0,8},{8,16},{16,24},{24,32},{32,40},{40,48},{48,56},{56,64},{64,7... | collective-permute-start | bytes 584 | tf_op jit(solution)/shard_map/ppermute | solution.py:19
  372.0 227.5 %reduce-scatter.4.cloned.1.call-start = ((), (), s32[]{:S(2)}) async-start(), calls=%async_computation.5 | async-start | bytes 14155776
  394.7 0.7 copy-start.6
Sparse Core Ops, SparseCore 0:
  9.9 47.7 all-gather.1
  372.1 149.1 all-reduce.2
  524.1 75.4 reduce-scatter.3
where the time goes:
time: 610 us; the launch traced here: 609 us
  waiting for transfers between devices  230 us (38%)
  local copies, waits for them, and re-layouts  199 us (33%)
  other arithmetic  115 us (19%)
  starting transfers between devices  35 us (6%)
  matrix products  15.7 us (3%)
  between operations  14.7 us (2%)
    unnamed x5, waiting for transfers between devices  202 us
    slice x4, local copies, waits for them, and re-layouts, shards(): extended[:, offset:offset + local_len:2]  112 us
    scatter-add x1, other arithmetic, shards(): running.at[:, got_rows.reshape(-1)]  59.1 us
    gather x2, local copies, waits for them, and re-layouts, shards(): fetched = jnp.take(activation, got_rows[0], axis=1)  32.5 us
    scatter-add x1, other arithmetic, shards(): running = running.at[:, donor_row].add(acceptor_vals * factor[None, :])  25.5 us
    all_to_all x1, waiting for transfers between devices, shards(): lax.all_to_all(fetched, 'pos', split_axis=1, concat_axis=1, tiled=True)  24.8 us
    unnamed x20, local copies, waits for them, and re-layouts  20.7 us
    scatter x1, other arithmetic, shards(): term_buffer = jnp.zeros((chan_local, pos_count * capacity), jnp.bfloat16)...  15 us
  transfers between devices with their start and end apart: 8, of which 4 were waited for; matrix products, arithmetic and copies ran while one was open for 52% of the time, Pallas kernels for 0%

commit v1 on v0

--- a/solution.py
+++ b/solution.py
@@ -1,25 +1,231 @@
+import functools
 import math
 
 import jax
 import jax.numpy as jnp
 from jax import lax
+from jax.experimental import pallas as pl
+from jax.experimental.pallas import tpu as pltpu
 from jax.sharding import PartitionSpec as P
 
 C = 768
 KERNEL = 4
-
-
-def extended_2(x, sides, width):
-    for axis, dim in sides:
-        devices, length = (lax.axis_size(axis), x.shape[dim])
-        up = [(i, (i + 1) % devices) for i in range(devices - 1)]
-        down = [(j, i) for i, j in up]
-        last = lax.slice_in_dim(x, length - width, length, axis=dim)
-        initial = lax.slice_in_dim(x, 0, width, axis=dim)
-        before = lax.ppermute(last, axis, up)
-        after = lax.ppermute(initial, axis, down)
-        x = jnp.concatenate([before, x, after], axis=dim)
-    return x
+BF = jnp.bfloat16
+F32 = jnp.float32
+MESH = pl.DeviceIdType.MESH
+NT = (((1,), (1,)), ((), ()))
+PARTS = 4
+
+
+def tail_kernel(
+    peers, ring, chan, total,
+    even_ref, odd_ref, wt_ref, full_hbm,
+    coarse_ref, weight_ref,
+    full, taps, halo_even, halo_odd, pair_out, pair_in, part, relay, before, after,
+    weight_acc, weight_out, weight_in,
+    full_sem, halo_send, halo_recv, pair_send, pair_recv, relay_send, relay_recv,
+    direct_send, direct_recv, sum_send, sum_recv, weight_send, weight_recv,
+):
+    me = lax.axis_index("pos")
+    ch = lax.axis_index("ch")
+    core = lax.rem(ch, 2)
+    row = ch // 2
+    sibling = ch + 1 - 2 * core
+    up = lax.rem(ch + 2, 2 * ring)
+    down = lax.rem(ch + 2 * ring - 2, 2 * ring)
+    row_up, row_down = lax.rem(row + 1, ring), lax.rem(row + ring - 1, ring)
+    row_far = lax.rem(row + 2, ring)
+    wide = even_ref.shape[1]
+    piece = wide // PARTS
+    rows_in = weight_ref.shape[0]
+    pos_up, pos_down = lax.rem(me + 1, peers), lax.rem(me + peers - 1, peers)
+
+    load_full = pltpu.make_async_copy(full_hbm, full, full_sem)
+    load_full.start()
+
+    barrier = pltpu.get_barrier_semaphore()
+
+    def greet(off, carry):
+        pl.semaphore_signal(barrier, inc=1, device_id={"pos": lax.rem(me + off, peers)}, device_id_type=MESH)
+        return carry
+
+    lax.fori_loop(1, peers, greet, 0)
+    for other in (sibling, up, down):
+        pl.semaphore_signal(barrier, inc=1, device_id={"ch": other}, device_id_type=MESH)
+    pl.semaphore_wait(barrier, peers + 2)
+
+    edge = halo_even.shape[1]
+    to_up = pltpu.make_async_remote_copy(
+        odd_ref.at[:, pl.ds(wide - edge, edge)], halo_odd, halo_send.at[0], halo_recv.at[0],
+        device_id={"pos": pos_up}, device_id_type=MESH)
+    to_down = pltpu.make_async_remote_copy(
+        even_ref.at[:, pl.ds(0, edge)], halo_even, halo_send.at[1], halo_recv.at[1],
+        device_id={"pos": pos_down}, device_id_type=MESH)
+    to_up.start()
+    to_down.start()
+    taps[pl.ds(chan, chan), :] = even_ref[...]
+    taps[pl.ds(2 * chan, chan), :] = odd_ref[...]
+    spot = lax.broadcasted_iota(jnp.int32, (chan, wide), 1)
+    moved_odd = pltpu.roll(odd_ref[...].astype(F32), 1, 1)
+    moved_even = pltpu.roll(even_ref[...].astype(F32), wide - 1, 1)
+    to_up.wait()
+    to_down.wait()
+    first = halo_odd[...].astype(F32)[:, edge - 1:edge] * jnp.where(me == 0, 0.0, 1.0)
+    last = halo_even[...].astype(F32)[:, 0:1] * jnp.where(me == peers - 1, 0.0, 1.0)
+    taps[pl.ds(0, chan), :] = jnp.where(spot == 0, first, moved_odd).astype(BF)
+    taps[pl.ds(3 * chan, chan), :] = jnp.where(spot == wide - 1, last, moved_even).astype(BF)
+
+    half = ring * chan
+
+    def pair_copy(q):
+        return pltpu.make_async_remote_copy(
+            pair_out.at[q], pair_in.at[q], pair_send.at[q], pair_recv.at[q],
+            device_id={"ch": sibling}, device_id_type=MESH)
+
+    def relay_copy(q):
+        return pltpu.make_async_remote_copy(
+            part.at[q, row_far], relay.at[q], relay_send.at[q], relay_recv.at[q],
+            device_id={"ch": up if q < PARTS // 2 else down}, device_id_type=MESH)
+
+    def direct_copy(q):
+        rising = q >= PARTS // 2
+        return pltpu.make_async_remote_copy(
+            part.at[q, row_up if rising else row_down], (before if rising else after).at[q],
+            direct_send.at[q], direct_recv.at[q],
+            device_id={"ch": up if rising else down}, device_id_type=MESH)
+
+    def sum_copy(q):
+        rising = q < PARTS // 2
+        return pltpu.make_async_remote_copy(
+            part.at[q, row_up if rising else row_down], (before if rising else after).at[q],
+            sum_send.at[q], sum_recv.at[q],
+            device_id={"ch": up if rising else down}, device_id_type=MESH)
+
+    order = (0, PARTS // 2, 1, PARTS // 2 + 1)
+    for q in order:
+        block = taps[:, q * piece:(q + 1) * piece]
+        pair_out[q] = jnp.dot(
+            wt_ref[pl.ds((1 - core) * half, half), :], block, preferred_element_type=F32
+        ).astype(BF).reshape(ring, chan, piece)
+        pair_copy(q).start()
+    for q in order:
+        block = taps[:, q * piece:(q + 1) * piece]
+        mine = jnp.dot(wt_ref[pl.ds(core * half, half), :], block, preferred_element_type=F32)
+        pair_copy(q).wait_recv()
+        both = mine.reshape(ring, chan, piece) + pair_in[q].astype(F32)
+        part[q] = both.astype(BF)
+        relay_copy(q).start()
+    for q in order:
+        direct_copy(q).start()
+
+    load_full.wait()
+    for q in range(PARTS):
+        where = slice(q * piece, (q + 1) * piece)
+        term = lax.dot_general(full[:, where], taps[:, where], NT, preferred_element_type=F32)
+        if q == 0:
+            weight_acc[...] = term
+        else:
+            weight_acc[...] += term
+    kept = weight_out.shape[1]
+    for p in range(peers):
+        weight_out[p] = jnp.concatenate(
+            [weight_acc[p * rows_in:(p + 1) * rows_in, :],
+             jnp.zeros((kept - rows_in, weight_acc.shape[1]), F32)], axis=0).astype(BF)
+
+    def weight_copy(off):
+        other = lax.rem(me + off, peers)
+        return pltpu.make_async_remote_copy(
+            weight_out.at[other], weight_in.at[me], weight_send.at[other], weight_recv.at[me],
+            device_id={"pos": other}, device_id_type=MESH)
+
+    def weight_start(off, carry):
+        weight_copy(off).start()
+        return carry
+
+    lax.fori_loop(1, peers, weight_start, 0)
+
+    for q in order:
+        rising = q < PARTS // 2
+        relay_copy(q).wait_recv()
+        goal = row_up if rising else row_down
+        part[q, goal] = (part[q, goal].astype(F32) + relay[q].astype(F32)).astype(BF)
+        sum_copy(q).start()
+    for q in order:
+        direct_copy(q).wait_recv()
+        sum_copy(q).wait_recv()
+        coarse_ref[:, q * piece:(q + 1) * piece] = (
+            part[q, row].astype(F32) + before[q].astype(F32) + after[q].astype(F32)).astype(BF)
+
+    own = weight_out[me]
+    weight_acc[pl.ds(0, kept), :] = own.astype(F32)
+
+    def weight_add(off, carry):
+        source = lax.rem(me + peers - off, peers)
+        pltpu.make_async_remote_copy(
+            weight_out.at[source], weight_in.at[source], weight_send.at[source], weight_recv.at[source],
+            device_id={"pos": source}, device_id_type=MESH).wait_recv()
+        weight_acc[pl.ds(0, kept), :] += weight_in[source].astype(F32)
+        return carry
+
+    lax.fori_loop(1, peers, weight_add, 0)
+    weight_ref[...] = weight_acc[0:rows_in, :] * (1.0 / math.sqrt(total))
+
+    for q in order:
+        pair_copy(q).wait_send()
+        relay_copy(q).wait_send()
+        direct_copy(q).wait_send()
+        sum_copy(q).wait_send()
+
+    def weight_sent(off, carry):
+        weight_copy(off).wait_send()
+        return carry
+
+    lax.fori_loop(1, peers, weight_sent, 0)
+
+
+def tail(even, odd, wt, full, peers, ring, chan, total):
+    wide = even.shape[1]
+    piece = wide // PARTS
+    channels = full.shape[0]
+    rows_in = channels // peers
+    kept = -(-rows_in // 16) * 16
+    outs = KERNEL * chan
+    edge = min(128, wide)
+    dma = pltpu.SemaphoreType.DMA
+    vmem = pl.BlockSpec(memory_space=pltpu.VMEM)
+    return pl.pallas_call(
+        functools.partial(tail_kernel, peers, ring, chan, total),
+        out_shape=(jax.ShapeDtypeStruct((chan, wide), BF), jax.ShapeDtypeStruct((rows_in, outs), F32)),
+        in_specs=[vmem, vmem, vmem, pl.BlockSpec(memory_space=pl.ANY)],
+        out_specs=(vmem, vmem),
+        scratch_shapes=[
+            pltpu.VMEM((channels, wide), BF),
+            pltpu.VMEM((outs, wide), BF),
+            pltpu.VMEM((chan, edge), BF),
+            pltpu.VMEM((chan, edge), BF),
+            pltpu.VMEM((PARTS, ring, chan, piece), BF),
+            pltpu.VMEM((PARTS, ring, chan, piece), BF),
+            pltpu.VMEM((PARTS, ring, chan, piece), BF),
+            pltpu.VMEM((PARTS, chan, piece), BF),
+            pltpu.VMEM((PARTS, chan, piece), BF),
+            pltpu.VMEM((PARTS, chan, piece), BF),
+            pltpu.VMEM((channels, outs), F32),
+            pltpu.VMEM((peers, kept, outs), BF),
+            pltpu.VMEM((peers, kept, outs), BF),
+            dma, dma((2,)), dma((2,)), dma((PARTS,)), dma((PARTS,)), dma((PARTS,)), dma((PARTS,)),
+            dma((PARTS,)), dma((PARTS,)), dma((PARTS,)), dma((PARTS,)), dma((peers,)), dma((peers,)),
+        ],
+        compiler_params=pltpu.CompilerParams(
+            collective_id=1, has_side_effects=True, vmem_limit_bytes=56 * 1024 * 1024),
+        cost_estimate=pl.CostEstimate(flops=4 * channels * outs * wide, bytes_accessed=2 * channels * wide * 2, transcendentals=0),
+        name="tail",
+    )(even, odd, wt, full)
+
+
+def split_weight(tap_weight, ring, chan):
+    taps, chan_local, channels = tap_weight.shape
+    table = tap_weight.reshape(taps * chan_local, ring, 2, chan)
+    return table.transpose(2, 1, 3, 0).reshape(channels, taps * chan_local)
 
 
 def shards(
@@ -32,6 +238,9 @@
     acceptor_owner,
     acceptor_row,
 ):
+    ring = lax.axis_size("ch") // 2
+    full_in = lax.all_gather(coarse_in, "ch", axis=0, tiled=True)
+    wt = split_weight(tap_weight, ring, track_grad.shape[0])
     chan_local, local_len = track_grad.shape
     junc_count = score_grad.shape[0]
     pos_count = lax.axis_size("pos")
@@ -67,27 +276,19 @@
         got_terms.reshape(chan_local, -1).astype(jnp.float32)
     )
     skip_grad = running.astype(jnp.bfloat16)
-    extended = extended_2(skip_grad, (("pos", 1),), 1)
-    tap_stack = jnp.stack(
-        [extended[:, offset : offset + local_len : 2] for offset in range(KERNEL)]
-    )
-    full_in = lax.all_gather(coarse_in, "ch", axis=0, tiled=True)
-    summed = lax.psum_scatter(
-        jnp.einsum("ip,kop->iko", full_in, tap_stack, preferred_element_type=jnp.float32),
-        "pos",
-        scatter_dimension=0,
-        tiled=True,
-    )
-    coarse_total = coarse_in.shape[1] * pos_count
-    weight_grad = (summed.transpose(1, 2, 0) * (1.0 / math.sqrt(coarse_total))).astype(jnp.bfloat16)
-    coarse_grad = lax.psum_scatter(
-        jnp.einsum("koi,kop->ip", tap_weight, tap_stack, preferred_element_type=jnp.float32),
-        "ch",
-        scatter_dimension=0,
-        tiled=True,
-    ).astype(jnp.bfloat16)
+    order = jnp.arange(256)
+    place = jnp.where(order % 2 == 0, order // 2, 128 + order // 2)
+    pick = (place[:, None] == order[None, :]).astype(BF)
+    split = jnp.einsum(
+        "cbt,tu->cbu", skip_grad.reshape(chan_local, local_len // 256, 256), pick, preferred_element_type=F32
+    ).astype(BF)
+    even = split[:, :, :128].reshape(chan_local, local_len // 2)
+    odd = split[:, :, 128:].reshape(chan_local, local_len // 2)
+    coarse_grad, weight_rows = tail(
+        even, odd, wt, full_in, pos_count, ring, chan_local, coarse_in.shape[1] * pos_count
+    )
+    weight_grad = weight_rows.reshape(-1, KERNEL, chan_local).transpose(1, 2, 0).astype(BF)
     return (skip_grad, coarse_grad, weight_grad)
-
 
 def solution(mesh):
     in_specs = (

time: 610 us -> 312 us (0.51)
  waiting for transfers between devices: 230 us -> 29.1 us
  local copies, waits for them, and re-layouts: 199 us -> 71.4 us
  Pallas kernels: 0 us -> 62.4 us
  matrix products: 15.7 us -> 2.05 us
  other arithmetic: 115 us -> 103 us
    unnamed x5 -> x1, waiting for transfers between devices: 202 us -> 0.68 us
    slice x6 -> x2, local copies, waits for them, and re-layouts: 112 us -> 0.4 us  [the longest x1 0.27 us: shards(): odd = split[:, :, 128:].reshape(chan_local, local_len // 2)]
    pallas_call x0 -> x1, Pallas kernels: none -> 62.4 us  [tail(): pl.pallas_call(functools.partial(tail_kernel, peers, ring, chan, total),...]
    scatter-add x1, other arithmetic: 59.1 us -> 45.4 us  [shards(): running.at[:, got_rows.reshape(-1)]]
    dot_general x2 -> x1, matrix products: 15.7 us -> 2.05 us  [shards(): jnp.einsum('cbt,tu->cbu', skip_grad.reshape(chan_local, local_len // 256,...]
    unnamed x20 -> x13, local copies, waits for them, and re-layouts: 20.7 us -> 8.04 us
  transfers between devices with their start and end apart: 8 -> 4, of which waited for: 4 -> 2; matrix products, arithmetic and copies ran while one was open for 52% -> 55% of each run, Pallas kernels for 0% -> 0%
where the time goes in v1:
time: 312 us; the launch traced here: 311 us
  other arithmetic  103 us (33%)
  local copies, waits for them, and re-layouts  71.4 us (23%)
  Pallas kernels  62.4 us (20%)
  starting transfers between devices  29.2 us (9%)
  waiting for transfers between devices  29.1 us (9%)
  between operations  14.3 us (5%)
    pallas_call x1, Pallas kernels, tail(): pl.pallas_call(functools.partial(tail_kernel, peers, ring, chan, total),...  62.4 us
    scatter-add x1, other arithmetic, shards(): running.at[:, got_rows.reshape(-1)]  45.4 us
    gather x2, local copies, waits for them, and re-layouts, shards(): fetched = jnp.take(activation, got_rows[0], axis=1)  32.6 us
    all_to_all x1, waiting for transfers between devices, shards(): lax.all_to_all(fetched, 'pos', split_axis=1, concat_axis=1, tiled=True)  25.6 us
    scatter-add x1, other arithmetic, shards(): running = running.at[:, donor_row].add(acceptor_vals * factor[None, :])  25.5 us
    scatter x1, other arithmetic, shards(): term_buffer = jnp.zeros((chan_local, pos_count * capacity), jnp.bfloat16)...  15 us
    all_to_all x1, starting transfers between devices, shards(): lax.all_to_all(request_rows, 'pos', split_axis=1, concat_axis=1, tiled=True)  11.9 us
    all_to_all x1, starting transfers between devices, shards(): lax.all_to_all(term_buffer, 'pos', split_axis=1, concat_axis=1, tiled=True)  9.33 us
  transfers between devices with their start and end apart: 4, of which 2 were waited for; matrix products, arithmetic and copies ran while one was open for 55% of the time, Pallas kernels for 0%

profile of v1, /device:TPU:1, one launch (start us, length us, event | category | flops | bytes accessed | tf_op | source)
XLA Modules:
  0.0 311.0 jit_solution(667882353743290234)
XLA Ops:
  7.2 0.0 copy-start.2
  7.2 0.0 copy-start.4
  7.2 0.0 copy-start.3
  7.2 0.0 all-gather.2.cloned.1.call-start
  7.2 0.7 all-gather.2.cloned.1.call-update
  7.9 0.7 fusion.12
  8.6 9.1 %reduce-window.6 = s32[32,16,128]{2,1,0:T(8,128)S(1)} reduce-window(s32[32,16,128]{2,1,0:T(8,128)S(1)} %fusion.12, s32[]{:T(128)} %constant.68.clone.1), window={size=1x1x128 pad=0_0x0_0x127_0}, to_apply=%region_0.0 | reduce-window | flops 8323072 | bytes 524292 | tf_op jit(solution)/shard_map/reduce-window
  17.7 0.1 slice.22
  17.9 0.2 copy.67
  18.1 0.2 reduce-window.9
  18.3 0.1 add_add_fusion
  18.4 0.0 copy-done.2
  18.5 0.1 fusion.10
  18.6 0.1 fusion.20
  18.6 8.8 %scatter_custom_fusion = s32[8192]{0:T(1024)} fusion(s32[2048]{0:T(1024)S(1)} %bitcast.75, s32[2048]{0:T(1024)} %param.15, s32[]{:T(128)} %constant.68.clone.1), kind=kCustom, calls=%fused_computation.43 | custom fusion | bytes 33280 | tf_op jit(solution)/shard_map/scatter | solution.py:257
  27.4 11.9 %all-to-all-start = ((s32[1,32,256]{2,0,1:T(1,128)}), s32[1,32,256]{2,0,1:T(1,128)S(1)}, u32[]{:S(2)}, u32[]{:S(2)}) async-start(s32[1,32,256]{2,0,1:T(1,128)} %bitcast.7), calls=%async_computation | async-start | bytes 65536 | tf_op jit(solution)/shard_map/all_to_all | solution.py:268
  39.3 0.0 copy-done.4
  39.3 0.0 copy-done.3
  39.4 3.2 %copy.55 = bf16[96,8192]{0,1:T(8,128)(2,1)S(1)} copy(bf16[96,8192]{1,0:T(8,128)(2,1)} %param.9) | data formatting | bytes 3145728 | tf_op args[1]
  42.6 15.0 %scatter_custom_fusion.2 = bf16[96,8192]{0,1:T(8,128)(2,1)} fusion(s32[2048]{0:T(1024)S(1)} %bitcast.76, bf16[]{:T(256)} %constant.76.clone.1, f32[2048]{0:T(1024)S(1)} %broadcast_multiply_fusion, pred[2048]{0:T(1024)(128)(4,1)S(1)} %compare_and_fusion.1, bf16[]{:T(256)} %constant.73.clone.1, bf16[96,8192]{0,1:T(8,128)(2,1)S(1)} %copy.55, ...), kind=kCustom, calls=%fused_computation.14 | custom fusion | flops 786432 | bytes 3688452 | tf_op jit(solution)/shard_map/scatter | solution.py:265
  57.6 3.9 %copy.60 = bf16[96,32,256]{2,0,1:T(8,128)(2,1)} copy(bf16[96,32,256]{0,2,1:T(8,128)(2,1)} %bitcast.58) | data formatting | bytes 3145728 | tf_op jit(solution)/shard_map/reshape | solution.py:266
  61.5 0.0 all-to-all-done
  61.5 9.3 %all-to-all-start.2 = ((bf16[96,32,256]{2,0,1:T(8,128)(2,1)}), bf16[96,32,256]{2,0,1:T(8,128)(2,1)}, u32[]{:S(2)}, u32[]{:S(2)}) async-start(bf16[96,32,256]{2,0,1:T(8,128)(2,1)} %copy.60), calls=%async_computation.2 | async-start | bytes 3145728 | tf_op jit(solution)/shard_map/all_to_all | solution.py:271
  70.9 29.4 %gather_fusion = bf16[8192,96]{1,0:T(8,128)(2,1)} fusion(bf16[96,8192]{0,1:T(8,128)(2,1)S(1)} %copy.55, s32[8192]{0:T(1024)S(1)} %broadcast_clamp_fusion), kind=kCustom, calls=%fused_computation | custom fusion | bytes 3178496 | tf_op jit(solution)/shard_map/jit(_take)/gather | solution.py:269
  100.4 3.1 %copy.56 = bf16[32,256,96]{1,2,0:T(8,128)(2,1)S(1)} copy(bf16[32,256,96]{2,1,0:T(8,128)(2,1)} %bitcast.59) | data formatting | bytes 3145728 | tf_op jit(solution)/shard_map/jit(_take)/gather | solution.py:269
  103.5 1.3 select_bitcast_fusion
  104.8 0.0 copy-start
  104.8 2.8 all-to-all-done.2
  107.7 7.9 %all-to-all-start.1 = ((bf16[96,32,256]{2,0,1:T(8,128)(2,1)}), bf16[96,32,256]{2,0,1:T(8,128)(2,1)}, u32[]{:S(2)}, u32[]{:S(2)}) async-start(bf16[96,32,256]{2,0,1:T(8,128)(2,1)} %select_bitcast_fusion), calls=%async_computation.1 | async-start | bytes 3145728 | tf_op jit(solution)/shard_map/all_to_all | solution.py:270
  115.6 0.0 copy-done
  115.6 0.0 copy-start.1
  115.6 2.9 copy.58
  118.5 0.0 copy-done.1
  118.5 0.8 reshape.165
  119.3 1.8 copy.64
  121.2 1.8 convert_bitcast_fusion
  123.0 0.3 copy.69
  123.3 3.3 %copy.62 = f32[8192,96]{1,0:T(8,128)} copy(f32[8192,96]{0,1:T(8,128)S(1)} %bitcast.57) | data formatting | bytes 6291456 | tf_op jit(solution)/shard_map/convert_element_type | solution.py:276
  126.6 25.6 %all-to-all-done.1 = bf16[96,32,256]{2,0,1:T(8,128)(2,1)} async-done(((bf16[96,32,256]{2,0,1:T(8,128)(2,1)}), bf16[96,32,256]{2,0,1:T(8,128)(2,1)}, u32[]{:S(2)}, u32[]{:S(2)}) %all-to-all-start.1) | async-done | bytes 1572896 | tf_op jit(solution)/shard_map/all_to_all | solution.py:270
  152.2 3.1 copy.57
  155.3 25.5 %scatter_custom_fusion.1 = f32[96,8192]{0,1:T(8,128)} fusion(f32[96,8192]{0,1:T(8,128)} %copy.58, s32[2048]{0:T(1024)S(1)} %get-tuple-element.27, f32[2048]{0:T(1024)S(1)} %broadcast_multiply_fusion, bf16[96,32,256]{0,2,1:T(8,128)(2,1)S(1)} %copy.57, s32[2048]{0:T(1024)S(1)} %bitcast.72), kind=kCustom, calls=%fused_computation.11 | custom fusion | flops 589824 | bytes 5259264 | tf_op jit(solution)/shard_map/scatter-add | solution.py:274
  180.8 45.4 %scatter_fusion = f32[96,8192]{0,1:T(8,128)} fusion(f32[96,8192]{0,1:T(8,128)} %scatter_custom_fusion.1, s32[8192]{0:T(1024)S(1)} %bitcast.67, f32[8192,96]{1,0:T(8,128)} %copy.62), kind=kCustom, calls=%fused_computation.6 | custom fusion | flops 786432 | bytes 9469952 | tf_op jit(solution)/shard_map/scatter-add | solution.py:275
  226.2 2.4 convert_element_type.46
  228.6 2.8 copy.66
  231.4 2.7 copy.63
  234.0 2.1 convolution_convert_fusion
  236.1 0.3 fusion.27
  236.4 1.8 copy_bitcast_fusion
  238.2 0.0 all-gather.2.cloned.1.call-done.full_hbm
  238.2 62.4 %tail.1 = (bf16[96,4096]{1,0:T(8,128)(2,1)}, f32[24,384]{1,0:T(8,128)}) custom-call(bf16[96,4096]{1,0:T(8,128)(2,1)} %get-tuple-element.29.even_ref, bf16[96,4096]{1,0:T(8,128)(2,1)} %get-tuple-element.28.odd_ref, bf16[768,384]{1,0:T(8,128)(2,1)} %bitcast.64, bf16[768,4096]{1,0:T(8,128)(2,1)} %all-gather.2.cloned.1.call-done.full_hbm), custom_call_target="tpu_custom_call" | custom-call | flops 4831838208 | bytes 12582912 | tf_op jit(solution)/shard_map/tail/pallas_call | solution.py:196
  300.6 0.8 convert_element_type.48
  301.4 0.1 convert_element_type.49
  301.4 0.6 copy.80
  302.1 2.1 copy.84
  (8 shorter events, 0.1 us)
Async XLA Ops:
  7.2 11.3 %copy-start.2 = (s32[2048,1]{0,1:T(1,128)S(1)}, s32[2048,1]{0,1:T(1,128)}, u32[]{:S(2)}) copy-start(s32[2048,1]{0,1:T(1,128)} %param.14) | copy-start | bytes 24580
  7.2 32.1 %copy-start.4 = (f32[2048]{0:T(1024)S(1)}, f32[2048]{0:T(1024)}, u32[]{:S(2)}) copy-start(f32[2048]{0:T(1024)} %param.12) | copy-start | bytes 24580
  7.2 32.1 %copy-start.3 = (s32[2048]{0:T(1024)S(1)}, s32[2048]{0:T(1024)}, u32[]{:S(2)}) copy-start(s32[2048]{0:T(1024)} %param.13) | copy-start | bytes 24580
  7.2 231.0 %all-gather.2.cloned.1.call-start = ((), (), s32[]{:S(2)}) async-start(), calls=%async_computation.3 | async-start | bytes 7077888 | tf_op jit(solution)/shard_map/all_gather | solution.py:242
  27.4 34.1 %all-to-all-start = ((s32[1,32,256]{2,0,1:T(1,128)}), s32[1,32,256]{2,0,1:T(1,128)S(1)}, u32[]{:S(2)}, u32[]{:S(2)}) async-start(s32[1,32,256]{2,0,1:T(1,128)} %bitcast.7), calls=%async_computation | async-start | bytes 65536 | tf_op jit(solution)/shard_map/all_to_all | solution.py:268
  61.5 46.1 %all-to-all-start.2 = ((bf16[96,32,256]{2,0,1:T(8,128)(2,1)}), bf16[96,32,256]{2,0,1:T(8,128)(2,1)}, u32[]{:S(2)}, u32[]{:S(2)}) async-start(bf16[96,32,256]{2,0,1:T(8,128)(2,1)} %copy.60), calls=%async_computation.2 | async-start | bytes 3145728 | tf_op jit(solution)/shard_map/all_to_all | solution.py:271
  104.8 10.8 %copy-start = (bf16[96,8192]{1,0:T(8,128)(2,1)S(1)}, bf16[96,8192]{1,0:T(8,128)(2,1)}, u32[]{:S(2)}) copy-start(bf16[96,8192]{1,0:T(8,128)(2,1)} %param.8) | copy-start | bytes 4718596
  107.7 44.5 %all-to-all-start.1 = ((bf16[96,32,256]{2,0,1:T(8,128)(2,1)}), bf16[96,32,256]{2,0,1:T(8,128)(2,1)}, u32[]{:S(2)}, u32[]{:S(2)}) async-start(bf16[96,32,256]{2,0,1:T(8,128)(2,1)} %select_bitcast_fusion), calls=%async_computation.1 | async-start | bytes 3145728 | tf_op jit(solution)/shard_map/all_to_all | solution.py:270
  115.6 2.9 copy-start.1
Sparse Core Ops, SparseCore 0:
  9.9 47.6 all-gather.1

commit v2 on v1

--- a/solution.py
+++ b/solution.py
@@ -21,7 +21,7 @@
     peers, ring, chan, total,
     even_ref, odd_ref, wt_ref, full_hbm,
     coarse_ref, weight_ref,
-    full, taps, halo_even, halo_odd, pair_out, pair_in, part, relay, before, after,
+    full, taps, halo_even, halo_odd, pair_out, pair_in, part, exact, relay, before, after,
     weight_acc, weight_out, weight_in,
     full_sem, halo_send, halo_recv, pair_send, pair_recv, relay_send, relay_recv,
     direct_send, direct_recv, sum_send, sum_recv, weight_send, weight_recv,
@@ -113,6 +113,7 @@
         mine = jnp.dot(wt_ref[pl.ds(core * half, half), :], block, preferred_element_type=F32)
         pair_copy(q).wait_recv()
         both = mine.reshape(ring, chan, piece) + pair_in[q].astype(F32)
+        exact[q] = both
         part[q] = both.astype(BF)
         relay_copy(q).start()
     for q in order:
@@ -148,13 +149,13 @@
         rising = q < PARTS // 2
         relay_copy(q).wait_recv()
         goal = row_up if rising else row_down
-        part[q, goal] = (part[q, goal].astype(F32) + relay[q].astype(F32)).astype(BF)
+        part[q, goal] = (exact[q, goal] + relay[q].astype(F32)).astype(BF)
         sum_copy(q).start()
     for q in order:
         direct_copy(q).wait_recv()
         sum_copy(q).wait_recv()
         coarse_ref[:, q * piece:(q + 1) * piece] = (
-            part[q, row].astype(F32) + before[q].astype(F32) + after[q].astype(F32)).astype(BF)
+            exact[q, row] + before[q].astype(F32) + after[q].astype(F32)).astype(BF)
 
     own = weight_out[me]
     weight_acc[pl.ds(0, kept), :] = own.astype(F32)
@@ -206,6 +207,7 @@
             pltpu.VMEM((PARTS, ring, chan, piece), BF),
             pltpu.VMEM((PARTS, ring, chan, piece), BF),
             pltpu.VMEM((PARTS, ring, chan, piece), BF),
+            pltpu.VMEM((PARTS, ring, chan, piece), F32),
             pltpu.VMEM((PARTS, chan, piece), BF),
             pltpu.VMEM((PARTS, chan, piece), BF),
             pltpu.VMEM((PARTS, chan, piece), BF),
@@ -228,6 +230,276 @@
     return table.transpose(2, 1, 3, 0).reshape(channels, taps * chan_local)
 
 
+FOLD = 8
+
+
+def select_fold(prod, high, chan):
+    kept = jnp.where(high == 0, prod[0:chan], 0.0)
+    for g in range(1, FOLD):
+        kept = kept + jnp.where(high == g, prod[g * chan:(g + 1) * chan], 0.0)
+    return kept
+
+
+def hot(mask):
+    return jnp.where(mask, 1.0, 0.0).astype(BF)
+
+
+def junction_kernel(
+    peers, chan,
+    act_hbm, track_hbm, owner_ref, acceptor_ref, donor_ref, score_ref,
+    skip_ref, even_ref, odd_ref,
+    act, track, acc, within_hot, terms, stack, wide_out, back,
+    rows_out, rows_in, terms_out, terms_in, fetch_out, fetch_in,
+    load_sem, rows_send, rows_recv, terms_send, terms_recv, fetch_send, fetch_recv,
+):
+    me = lax.axis_index("pos")
+    count = owner_ref.shape[1]
+    cap = within_hot.shape[0]
+    fold = act.shape[1]
+    per = fold.bit_length() - 1
+
+    def load(which, hbm, ref, g):
+        return pltpu.make_async_copy(
+            hbm.at[:, pl.ds(g * fold, fold)], ref.at[pl.ds(g * chan, chan), :], load_sem.at[which, g])
+
+    for g in range(FOLD):
+        load(0, act_hbm, act, g).start()
+    for g in range(FOLD):
+        load(1, track_hbm, track, g).start()
+
+    barrier = pltpu.get_barrier_semaphore()
+
+    def greet(off, carry):
+        pl.semaphore_signal(barrier, inc=1, device_id={"pos": lax.rem(me + off, peers)}, device_id_type=MESH)
+        return carry
+
+    lax.fori_loop(1, peers, greet, 0)
+
+    owner = owner_ref[...]
+    named = jnp.where(owner == lax.broadcasted_iota(jnp.int32, (peers, count), 0), 1.0, 0.0)
+    earlier = hot(lax.broadcasted_iota(jnp.int32, (cap, cap), 0) < lax.broadcasted_iota(jnp.int32, (cap, cap), 1))
+    carried = jnp.zeros((peers, 1), F32)
+    for b in range(count // cap):
+        part = named[:, b * cap:(b + 1) * cap]
+        before = jnp.dot(part.astype(BF), earlier, preferred_element_type=F32) + carried
+        within = jnp.sum(part * before, axis=0, keepdims=True).astype(jnp.int32)
+        within_hot[:, b * cap:(b + 1) * cap] = hot(lax.broadcasted_iota(jnp.int32, (cap, cap), 0) == within)
+        carried = carried + jnp.sum(part, axis=1, keepdims=True)
+    wanted = acceptor_ref[...]
+    planes = jnp.concatenate(
+        [named * (wanted >> 7).astype(F32), named * (wanted & 127).astype(F32)], axis=0).astype(BF)
+    slots = lax.dot_general(planes, within_hot[...], NT, preferred_element_type=F32)
+    rows = (slots[0:peers] * 128.0 + slots[peers:2 * peers]).astype(jnp.int32)
+    for p in range(peers):
+        rows_out[p] = rows[p:p + 1, :]
+    rows_in[me] = rows_out[me]
+
+    pl.semaphore_wait(barrier, peers - 1)
+
+    def send(kind, other):
+        out, into, sent, got = (
+            (rows_out, rows_in, rows_send, rows_recv),
+            (terms_out, terms_in, terms_send, terms_recv),
+            (fetch_out, fetch_in, fetch_send, fetch_recv),
+        )[kind]
+        return pltpu.make_async_remote_copy(
+            out.at[other], into.at[me], sent.at[other], got.at[me],
+            device_id={"pos": other}, device_id_type=MESH)
+
+    def arrival(kind, other):
+        out, into, sent, got = (
+            (rows_out, rows_in, rows_send, rows_recv),
+            (terms_out, terms_in, terms_send, terms_recv),
+            (fetch_out, fetch_in, fetch_send, fetch_recv),
+        )[kind]
+        return pltpu.make_async_remote_copy(
+            out.at[other], into.at[other], sent.at[other], got.at[other],
+            device_id={"pos": other}, device_id_type=MESH)
+
+    def each(first, body):
+        def run(off, carry):
+            body(off)
+            return carry
+        lax.fori_loop(first, peers, run, 0)
+
+    each(1, lambda off: send(0, lax.rem(me + off, peers)).start())
+
+    def gather(where):
+        spot = lax.broadcasted_iota(jnp.int32, (fold, where.shape[1]), 0)
+        prod = jnp.dot(act[...], hot(spot == (where & (fold - 1))), preferred_element_type=F32)
+        return select_fold(prod, where >> per, chan)
+
+    for g in range(FOLD):
+        load(0, act_hbm, act, g).wait()
+
+    def make_terms(b, carry):
+        at = pl.ds(pl.multiple_of(b * cap, cap), cap)
+        factor = score_ref[:, at] * (1.0 / math.sqrt(C))
+        terms[:, at] = (gather(donor_ref[:, at]) * factor).astype(BF)
+        return carry
+
+    lax.fori_loop(0, count // cap, make_terms, 0)
+
+    GROUP = 8
+
+    def expand(group, carry):
+        for k in range(GROUP):
+            other = lax.rem(me + group * GROUP + k, peers)
+            stack[k * chan:(k + 1) * chan, :] = terms[...] * hot(owner_ref[...] == other)
+        slotted = lax.dot_general(stack[...], within_hot[...], NT, preferred_element_type=F32)
+        for k in range(GROUP):
+            other = lax.rem(me + group * GROUP + k, peers)
+            terms_out[other] = slotted[k * chan:(k + 1) * chan, :].astype(BF)
+        for k in range(GROUP):
+            other = lax.rem(me + group * GROUP + k, peers)
+
+            @pl.when(other != me)
+            def _():
+                send(1, other).start()
+        return carry
+
+    lax.fori_loop(0, peers // GROUP, expand, 0)
+    terms_in[me] = terms_out[me]
+
+    fetch_in[me] = gather(rows_in[me]).astype(BF)
+
+    def answer(off):
+        other = lax.rem(me + off, peers)
+        arrival(0, other).wait_recv()
+        fetch_out[other] = gather(rows_in[other]).astype(BF)
+        send(2, other).start()
+
+    each(1, answer)
+
+    acc[...] = jnp.zeros_like(acc)
+    step = min(256, fold)
+
+    def scatter(values, where):
+        n = where.shape[1]
+        high, low = where >> per, where & (fold - 1)
+        for g in range(FOLD):
+            wide_out[g * chan:(g + 1) * chan, :] = values * hot(high == g)
+        spot = lax.broadcasted_iota(jnp.int32, (step, n), 0)
+        for r in range(fold // step):
+            here = hot(spot + r * step == low)
+            acc[:, r * step:(r + 1) * step] += lax.dot_general(
+                wide_out[...], here, NT, preferred_element_type=F32)
+
+    batch = wide_out.shape[1] // cap
+
+    def add_terms(group, carry):
+        values, where = [], []
+        for k in range(batch):
+            other = lax.rem(me + peers - (group * batch + k), peers)
+
+            @pl.when(other != me)
+            def _():
+                arrival(1, other).wait_recv()
+            values.append(terms_in[other])
+            where.append(rows_in[other])
+        scatter(jnp.concatenate(values, axis=1), jnp.concatenate(where, axis=1))
+        return carry
+
+    lax.fori_loop(0, peers // batch, add_terms, 0)
+
+    back[...] = jnp.zeros_like(back)
+
+    def collect(group, carry):
+        blocks, names = [], []
+        for k in range(GROUP):
+            other = lax.rem(me + peers - (group * GROUP + k), peers)
+
+            @pl.when(other != me)
+            def _():
+                arrival(2, other).wait_recv()
+            blocks.append(fetch_in[other])
+            names.append(other)
+        block = jnp.concatenate(blocks, axis=0)
+        for b in range(count // cap):
+            at = slice(b * cap, (b + 1) * cap)
+            prod = jnp.dot(block, within_hot[:, at], preferred_element_type=F32)
+            owners = owner_ref[:, at]
+            kept = back[:, at]
+            for k in range(GROUP):
+                kept = kept + jnp.where(owners == names[k], prod[k * chan:(k + 1) * chan], 0.0)
+            back[:, at] = kept
+        return carry
+
+    lax.fori_loop(0, peers // GROUP, collect, 0)
+    width = batch * cap
+    for b in range(count // width):
+        at = slice(b * width, (b + 1) * width)
+        factor = score_ref[:, at] * (1.0 / math.sqrt(C))
+        scatter((back[:, at] * factor).astype(BF), donor_ref[:, at])
+
+    for g in range(FOLD):
+        load(1, track_hbm, track, g).wait()
+    pair = min(256, fold)
+    spot = lax.broadcasted_iota(jnp.int32, (pair, pair), 0)
+    goal = lax.broadcasted_iota(jnp.int32, (pair, pair), 1)
+    half = pair // 2
+    pick = hot(spot == jnp.where(goal < half, 2 * goal, 2 * (goal - half) + 1))
+    for q in range(fold // pair):
+        at = slice(q * pair, (q + 1) * pair)
+        skip = (track[:, at].astype(F32) + acc[:, at]).astype(BF)
+        split = jnp.dot(skip, pick, preferred_element_type=F32).astype(BF)
+        for g in range(FOLD):
+            rows_of = slice(g * chan, (g + 1) * chan)
+            skip_ref[:, g * fold + q * pair:g * fold + (q + 1) * pair] = skip[rows_of]
+            start = (g * fold + q * pair) // 2
+            even_ref[:, start:start + half] = split[rows_of, :half]
+            odd_ref[:, start:start + half] = split[rows_of, half:]
+
+    def drain(off):
+        other = lax.rem(me + off, peers)
+        for kind in range(3):
+            send(kind, other).wait_send()
+
+    each(1, drain)
+
+
+def junctions(activation, track_grad, owner, acceptor_row, donor_row, score_grad, peers):
+    chan, length = activation.shape
+    count = owner.shape[1]
+    cap = count // 8
+    fold = length // FOLD
+    dma = pltpu.SemaphoreType.DMA
+    vmem = pl.BlockSpec(memory_space=pltpu.VMEM)
+    hbm = pl.BlockSpec(memory_space=pl.ANY)
+    return pl.pallas_call(
+        functools.partial(junction_kernel, peers, chan),
+        out_shape=(
+            jax.ShapeDtypeStruct((chan, length), BF),
+            jax.ShapeDtypeStruct((chan, length // 2), BF),
+            jax.ShapeDtypeStruct((chan, length // 2), BF),
+        ),
+        in_specs=[hbm, hbm, vmem, vmem, vmem, vmem],
+        out_specs=(vmem, vmem, vmem),
+        scratch_shapes=[
+            pltpu.VMEM((FOLD * chan, fold), BF),
+            pltpu.VMEM((FOLD * chan, fold), BF),
+            pltpu.VMEM((FOLD * chan, fold), F32),
+            pltpu.VMEM((cap, count), BF),
+            pltpu.VMEM((chan, count), BF),
+            pltpu.VMEM((8 * chan, count), BF),
+            pltpu.VMEM((FOLD * chan, 4 * cap), BF),
+            pltpu.VMEM((chan, count), F32),
+            pltpu.VMEM((peers, 1, cap), jnp.int32),
+            pltpu.VMEM((peers, 1, cap), jnp.int32),
+            pltpu.VMEM((peers, chan, cap), BF),
+            pltpu.VMEM((peers, chan, cap), BF),
+            pltpu.VMEM((peers, chan, cap), BF),
+            pltpu.VMEM((peers, chan, cap), BF),
+            dma((2, FOLD)),
+            dma((peers,)), dma((peers,)), dma((peers,)), dma((peers,)), dma((peers,)), dma((peers,)),
+        ],
+        compiler_params=pltpu.CompilerParams(
+            collective_id=2, has_side_effects=True, vmem_limit_bytes=56 * 1024 * 1024),
+        cost_estimate=pl.CostEstimate(flops=96 * 8 * 1024 * 256 * 768, bytes_accessed=8 * chan * length, transcendentals=0),
+        name="junctions",
+    )(activation, track_grad, owner, acceptor_row, donor_row, score_grad)
+
+
 def shards(
     track_grad,
     activation,
@@ -238,54 +510,21 @@
     acceptor_owner,
     acceptor_row,
 ):
-    ring = lax.axis_size("ch") // 2
+    peers, ring = lax.axis_size("pos"), lax.axis_size("ch") // 2
+    chan_local = track_grad.shape[0]
     full_in = lax.all_gather(coarse_in, "ch", axis=0, tiled=True)
-    wt = split_weight(tap_weight, ring, track_grad.shape[0])
-    chan_local, local_len = track_grad.shape
-    junc_count = score_grad.shape[0]
-    pos_count = lax.axis_size("pos")
-    capacity = junc_count // 8
-    factor = score_grad * (1.0 / math.sqrt(C))
-    owners = acceptor_owner[:, 0]
-    members = (owners[:, None] == jnp.arange(pos_count, dtype=jnp.int32)[None, :]).astype(jnp.int32)
-    rank_list = jnp.cumsum(members, axis=0) - 1
-    within = jnp.sum(rank_list * members, axis=1)
-    flat_slot = owners * capacity + within
-    request_rows = (
-        jnp.zeros((pos_count * capacity,), jnp.int32)
-        .at[flat_slot]
-        .set(acceptor_row)
-        .reshape(1, pos_count, capacity)
+    wt = split_weight(tap_weight, ring, chan_local)
+    skip_grad, even, odd = junctions(
+        activation,
+        track_grad,
+        acceptor_owner.reshape(1, -1),
+        acceptor_row.reshape(1, -1),
+        donor_row.reshape(1, -1),
+        score_grad.reshape(1, -1),
+        peers,
     )
-    donor_vals = jnp.take(activation, donor_row, axis=1).astype(jnp.float32)
-    acceptor_terms = (donor_vals * factor[None, :]).astype(jnp.bfloat16)
-    term_buffer = (
-        jnp.zeros((chan_local, pos_count * capacity), jnp.bfloat16)
-        .at[:, flat_slot]
-        .set(acceptor_terms)
-        .reshape(chan_local, pos_count, capacity)
-    )
-    got_rows = lax.all_to_all(request_rows, "pos", split_axis=1, concat_axis=1, tiled=True)
-    fetched = jnp.take(activation, got_rows[0], axis=1)
-    returned = lax.all_to_all(fetched, "pos", split_axis=1, concat_axis=1, tiled=True)
-    got_terms = lax.all_to_all(term_buffer, "pos", split_axis=1, concat_axis=1, tiled=True)
-    acceptor_vals = returned[:, owners, within].astype(jnp.float32)
-    running = track_grad.astype(jnp.float32)
-    running = running.at[:, donor_row].add(acceptor_vals * factor[None, :])
-    running = running.at[:, got_rows.reshape(-1)].add(
-        got_terms.reshape(chan_local, -1).astype(jnp.float32)
-    )
-    skip_grad = running.astype(jnp.bfloat16)
-    order = jnp.arange(256)
-    place = jnp.where(order % 2 == 0, order // 2, 128 + order // 2)
-    pick = (place[:, None] == order[None, :]).astype(BF)
-    split = jnp.einsum(
-        "cbt,tu->cbu", skip_grad.reshape(chan_local, local_len // 256, 256), pick, preferred_element_type=F32
-    ).astype(BF)
-    even = split[:, :, :128].reshape(chan_local, local_len // 2)
-    odd = split[:, :, 128:].reshape(chan_local, local_len // 2)
     coarse_grad, weight_rows = tail(
-        even, odd, wt, full_in, pos_count, ring, chan_local, coarse_in.shape[1] * pos_count
+        even, odd, wt, full_in, peers, ring, chan_local, coarse_in.shape[1] * peers
     )
     weight_grad = weight_rows.reshape(-1, KERNEL, chan_local).transpose(1, 2, 0).astype(BF)
     return (skip_grad, coarse_grad, weight_grad)

time: 312 us -> 163 us (0.52)
  other arithmetic: 103 us -> 0.77 us
  Pallas kernels: 62.4 us -> 141 us
  local copies, waits for them, and re-layouts: 71.4 us -> 5.84 us
  starting transfers between devices: 29.2 us -> 0.04 us
  waiting for transfers between devices: 29.1 us -> 0.68 us
    pallas_call x0 -> x1, Pallas kernels: none -> 94.9 us  [junctions(): pl.pallas_call(functools.partial(junction_kernel, peers, chan), out_shape...]
    scatter-add x2 -> x0, other arithmetic: 70.9 us -> none  [the longest x1 45.4 us: shards(): running.at[:, got_rows.reshape(-1)]]
    gather x2 -> x0, local copies, waits for them, and re-layouts: 32.6 us -> none  [shards(): fetched = jnp.take(activation, got_rows[0], axis=1)]
    all_to_all x3 -> x0, starting transfers between devices: 29.1 us -> none  [the longest x1 11.9 us: shards(): lax.all_to_all(request_rows, 'pos', split_axis=1, concat_axis=1, tiled=True)]
    all_to_all x3 -> x0, waiting for transfers between devices: 28.4 us -> none  [the longest x1 25.6 us: shards(): lax.all_to_all(fetched, 'pos', split_axis=1, concat_axis=1, tiled=True)]
    pallas_call x1, Pallas kernels: 62.4 us -> 46.3 us  [tail(): pl.pallas_call(functools.partial(tail_kernel, peers, ring, chan, total),...]
    scatter x1 -> x0, other arithmetic: 15 us -> none  [shards(): term_buffer = jnp.zeros((chan_local, pos_count * capacity), jnp.bfloat16)...]
    another operation x2 -> x0, other arithmetic: 9.27 us -> none
  transfers between devices with their start and end apart: 4 -> 1, of which waited for: 2 -> 0; matrix products, arithmetic and copies ran while one was open for 55% -> 2% of each run, Pallas kernels for 0% -> 58%
where the time goes in v2:
time: 163 us
  Pallas kernels  141 us (87%)
  between operations  14.1 us (9%)
  local copies, waits for them, and re-layouts  5.84 us (4%)
    pallas_call x1, Pallas kernels, junctions(): pl.pallas_call(functools.partial(junction_kernel, peers, chan), out_shape...  94.9 us
    pallas_call x1, Pallas kernels, tail(): pl.pallas_call(functools.partial(tail_kernel, peers, ring, chan, total),...  46.3 us
  transfers between devices with their start and end apart: 1, of which 0 were waited for; matrix products, arithmetic and copies ran while one was open for 2% of the time, Pallas kernels for 58%

profile of v2, /device:TPU:1, one launch (start us, length us, event | category | flops | bytes accessed | tf_op | source)
XLA Modules:
  0.0 162.6 jit_solution(6771801062567115702)
XLA Ops:
  7.2 0.0 all-gather.2.cloned.1.call-start
  7.2 0.7 all-gather.2.cloned.1.call-update
  7.9 0.0 copy-start.2
  7.9 94.9 %junctions.1 = (bf16[96,8192]{1,0:T(8,128)(2,1)}, bf16[96,4096]{1,0:T(8,128)(2,1)}, bf16[96,4096]{1,0:T(8,128)(2,1)}) custom-call(bf16[96,8192]{1,0:T(8,128)(2,1)} %act_hbm.1, bf16[96,8192]{1,0:T(8,128)(2,1)} %track_hbm.1, s32[1,2048]{1,0:T(1,128)} %bitcast.12, s32[1,2048]{1,0:T(1,128)} %bitcast.13, s32[1,2048]{1,0:T(1,128)} %bitcast.14, f32[1,2048]{1,0:T(1,128)} %bitcast.15), custom_call_target="tpu_custom_call" | custom-call | flops 154618822656 | bytes 6291456 | tf_op jit(solution)/shard_map/junctions/pallas_call | solution.py:469
  102.9 0.0 copy-done.2
  102.9 0.8 reshape.30
  103.7 1.8 %copy.13 = bf16[2,4,96,384]{3,2,1,0:T(8,128)(2,1)} copy(bf16[2,4,96,384]{2,0,1,3:T(2,128)(2,1)S(1)} %bitcast.9) | data formatting | bytes 1179648 | tf_op jit(solution)/shard_map/transpose | solution.py:230
  105.5 0.0 all-gather.2.cloned.1.call-done.full_hbm
  105.5 0.0 copy-start
  105.5 46.3 %tail.1 = (bf16[96,4096]{1,0:T(8,128)(2,1)}, f32[24,384]{1,0:T(8,128)}) custom-call(bf16[96,4096]{1,0:T(8,128)(2,1)} %get-tuple-element.9.even_ref, bf16[96,4096]{1,0:T(8,128)(2,1)} %get-tuple-element.10.odd_ref, bf16[768,384]{1,0:T(8,128)(2,1)} %bitcast.10, bf16[768,4096]{1,0:T(8,128)(2,1)} %all-gather.2.cloned.1.call-done.full_hbm), custom_call_target="tpu_custom_call" | custom-call | flops 4831838208 | bytes 12582912 | tf_op jit(solution)/shard_map/tail/pallas_call | solution.py:197
  151.7 0.8 convert_element_type.9
  152.5 0.1 convert_element_type.10
  152.6 0.6 copy.16
  153.2 0.0 copy-done
  153.2 0.0 copy-start.1
  153.2 1.1 copy.19
  154.3 0.5 copy-done.1
  154.9 0.9 copy.20
Async XLA Ops:
  7.2 98.3 %all-gather.2.cloned.1.call-start = ((), (), s32[]{:S(2)}) async-start(), calls=%async_computation | async-start | bytes 7077888 | tf_op jit(solution)/shard_map/all_gather | solution.py:515
  7.9 95.0 %copy-start.2 = (bf16[4,96,768]{2,1,0:T(8,128)(2,1)S(1)}, bf16[4,96,768]{2,1,0:T(8,128)(2,1)}, u32[]{:S(2)}) copy-start(bf16[4,96,768]{2,1,0:T(8,128)(2,1)} %param.11) | copy-start | bytes 1769476
  105.5 47.7 %copy-start = (bf16[96,8192]{1,0:T(8,128)(2,1)S(1)}, bf16[96,8192]{1,0:T(8,128)(2,1)}, u32[]{:S(2)}) copy-start(bf16[96,8192]{1,0:T(8,128)(2,1)} %get-tuple-element.16) | copy-start | bytes 4718596
  153.2 1.7 %copy-start.1 = (bf16[96,4096]{1,0:T(8,128)(2,1)S(1)}, bf16[96,4096]{1,0:T(8,128)(2,1)}, u32[]{:S(2)}) copy-start(bf16[96,4096]{1,0:T(8,128)(2,1)} %get-tuple-element.17) | copy-start | bytes 2359300
Sparse Core Ops, SparseCore 0:
  9.8 47.7 all-gather.1

commit v3 on v0

v3 whole, which is shorter than its diff:
```python
import functools
import math

import jax
import jax.numpy as jnp
from jax import lax
from jax.experimental import pallas as pl
from jax.experimental.pallas import tpu as pltpu
from jax.sharding import PartitionSpec as P

C = 768
KERNEL = 4
FOLD = 8
PARTS = 4
GROUP = 8
BATCH = 4
BF = jnp.bfloat16
F32 = jnp.float32
MESH = pl.DeviceIdType.MESH
NT = (((1,), (1,)), ((), ()))


def hot(mask):
    return jnp.where(mask, 1.0, 0.0).astype(BF)


def iota(shape, dim):
    return lax.broadcasted_iota(jnp.int32, shape, dim)


def section_kernel(
    peers, inner, ring, total,
    act_hbm, track_hbm, coarse_hbm, weight_in_ref, owner_ref, acceptor_ref, donor_ref, score_ref,
    skip_ref, coarse_ref, weight_ref,
    act, track, acc, within_hot, terms, stack, spread, back,
    rows_out, rows_in, terms_out, terms_in, fetch_out, fetch_in,
    full, wt, taps, halo_even, halo_odd, pair_out, pair_in, part, exact, relay, before, after,
    weight_acc, first_out, first_in, second_out, second_in,
    load_sem, rows_send, rows_recv, terms_send, terms_recv, fetch_send, fetch_recv,
    gather_send, gather_recv, halo_send, halo_recv, pair_send, pair_recv, relay_send, relay_recv,
    direct_send, direct_recv, sum_send, sum_recv, first_send, first_recv, second_send, second_recv,
):
    me = lax.axis_index("pos")
    ch = lax.axis_index("ch")
    outer = peers // inner
    mine_out, mine_in = me // inner, lax.rem(me, inner)
    core, row = lax.rem(ch, 2), ch // 2
    sibling = ch + 1 - 2 * core
    up = lax.rem(ch + 2, 2 * ring)
    down = lax.rem(ch + 2 * ring - 2, 2 * ring)
    far = lax.rem(ch + 4, 2 * ring)
    row_up, row_down = lax.rem(row + 1, ring), lax.rem(row + ring - 1, ring)
    row_far = lax.rem(row + 2, ring)
    chan, wide = coarse_ref.shape
    piece = wide // PARTS
    count = owner_ref.shape[1]
    cap = within_hot.shape[0]
    fold = act.shape[1]
    per = fold.bit_length() - 1
    channels = full.shape[0]
    rows_each = channels // peers

    def load(which, hbm, ref, g):
        return pltpu.make_async_copy(
            hbm.at[:, pl.ds(g * fold, fold)], ref.at[pl.ds(g * chan, chan), :], load_sem.at[which, g])

    for g in range(FOLD):
        load(0, act_hbm, act, g).start()
    for g in range(FOLD):
        load(1, track_hbm, track, g).start()
    own_rows = pl.ds(pl.multiple_of(ch * chan, chan), chan)
    load_coarse = pltpu.make_async_copy(coarse_hbm, full.at[own_rows, :], load_sem.at[2, 0])
    load_coarse.start()

    def each(first, body):
        def run(off, carry):
            body(off)
            return carry
        lax.fori_loop(first, peers, run, 0)

    barrier = pltpu.get_barrier_semaphore()
    each(1, lambda off: pl.semaphore_signal(
        barrier, inc=1, device_id={"pos": lax.rem(me + off, peers)}, device_id_type=MESH))
    for other in (sibling, up, down, far):
        pl.semaphore_signal(barrier, inc=1, device_id={"ch": other}, device_id_type=MESH)

    owner = owner_ref[...]
    named = jnp.where(owner == iota((peers, count), 0), 1.0, 0.0)
    blocks = count // cap
    stacked = jnp.concatenate([named[:, b * cap:(b + 1) * cap] for b in range(blocks)], axis=0)
    ranks = jnp.dot(stacked.astype(BF), hot(iota((cap, cap), 0) < iota((cap, cap), 1)), preferred_element_type=F32)
    sums = jnp.sum(stacked, axis=1, keepdims=True)
    carried = jnp.zeros((peers, 1), F32)
    for b in range(blocks):
        at = slice(b * peers, (b + 1) * peers)
        within = jnp.sum(stacked[at] * (ranks[at] + carried), axis=0, keepdims=True).astype(jnp.int32)
        within_hot[:, b * cap:(b + 1) * cap] = hot(iota((cap, cap), 0) == within)
        carried = carried + sums[at]
    wanted = acceptor_ref[...]
    planes = jnp.concatenate(
        [named * (wanted >> 7).astype(F32), named * (wanted & 127).astype(F32)], axis=0).astype(BF)
    slots = lax.dot_general(planes, within_hot[...], NT, preferred_element_type=F32)
    rows = (slots[0:peers] * 128.0 + slots[peers:2 * peers]).astype(jnp.int32)
    for p in range(peers):
        rows_out[p] = rows[p:p + 1, :]
    rows_in[me] = rows_out[me]

    pl.semaphore_wait(barrier, peers + 3)

    kinds = (
        (rows_out, rows_in, rows_send, rows_recv),
        (terms_out, terms_in, terms_send, terms_recv),
        (fetch_out, fetch_in, fetch_send, fetch_recv),
    )

    def send(kind, other):
        out, into, sent, got = kinds[kind]
        return pltpu.make_async_remote_copy(
            out.at[other], into.at[me], sent.at[other], got.at[me],
            device_id={"pos": other}, device_id_type=MESH)

    def arrival(kind, other):
        out, into, sent, got = kinds[kind]
        return pltpu.make_async_remote_copy(
            out.at[other], into.at[other], sent.at[other], got.at[other],
            device_id={"pos": other}, device_id_type=MESH)

    each(1, lambda off: send(0, lax.rem(me + off, peers)).start())

    def share(n, source, goal):
        span = pl.ds(pl.multiple_of(source * chan, chan), chan)
        return pltpu.make_async_remote_copy(
            coarse_hbm if n < 4 else full.at[span, :], full.at[span, :], gather_send.at[n], gather_recv.at[source],
            device_id={"ch": goal}, device_id_type=MESH)

    for n, goal in enumerate((up, down, far, sibling)):
        share(n, ch, goal).start()

    def shared(source):
        span = pl.ds(pl.multiple_of(source * chan, chan), chan)
        return pltpu.make_async_remote_copy(
            full.at[span, :], full.at[span, :], gather_send.at[0], gather_recv.at[source],
            device_id={"ch": sibling}, device_id_type=MESH)

    def gather(where):
        spot = iota((fold, where.shape[1]), 0)
        prod = jnp.dot(act[...], hot(spot == (where & (fold - 1))), preferred_element_type=F32)
        high = where >> per
        kept = jnp.where(high == 0, prod[0:chan], 0.0)
        for g in range(1, FOLD):
            kept = kept + jnp.where(high == g, prod[g * chan:(g + 1) * chan], 0.0)
        return kept

    for g in range(FOLD):
        load(0, act_hbm, act, g).wait()

    def make_terms(b, carry):
        at = pl.ds(pl.multiple_of(b * cap, cap), cap)
        factor = score_ref[:, at] * (1.0 / math.sqrt(C))
        terms[:, at] = (gather(donor_ref[:, at]) * factor).astype(BF)
        return carry

    lax.fori_loop(0, blocks, make_terms, 0)

    def answer(off):
        other = lax.rem(me + off, peers)
        arrival(0, other).wait_recv()
        fetch_out[other] = gather(rows_in[other]).astype(BF)
        send(2, other).start()

    each(1, answer)
    fetch_in[me] = gather(rows_in[me]).astype(BF)

    def expand(group, carry):
        for k in range(GROUP):
            other = lax.rem(me + group * GROUP + k, peers)
            stack[k * chan:(k + 1) * chan, :] = terms[...] * hot(owner_ref[...] == other)
        slotted = lax.dot_general(stack[...], within_hot[...], NT, preferred_element_type=F32)
        for k in range(GROUP):
            other = lax.rem(me + group * GROUP + k, peers)
            terms_out[other] = slotted[k * chan:(k + 1) * chan, :].astype(BF)

            @pl.when(other != me)
            def _():
                send(1, other).start()
        return carry

    lax.fori_loop(0, peers // GROUP, expand, 0)
    terms_in[me] = terms_out[me]

    for g in range(FOLD):
        load(1, track_hbm, track, g).wait()
    acc[...] = track[...].astype(F32)
    for k in range(KERNEL):
        turned = weight_in_ref[k].astype(F32).T.astype(BF)
        for r in range(ring):
            for c in range(2):
                wt[(c * ring + r) * chan:(c * ring + r + 1) * chan, k * chan:(k + 1) * chan] = (
                    turned[(2 * r + c) * chan:(2 * r + c + 1) * chan])
    back[...] = jnp.zeros_like(back)

    def collect(group, carry):
        held, names = [], []
        for k in range(GROUP):
            other = lax.rem(me + peers - (group * GROUP + k), peers)

            @pl.when(other != me)
            def _():
                arrival(2, other).wait_recv()
            held.append(fetch_in[other])
            names.append(other)
        block = jnp.concatenate(held, axis=0)
        for b in range(blocks):
            at = slice(b * cap, (b + 1) * cap)
            prod = jnp.dot(block, within_hot[:, at], preferred_element_type=F32)
            owners = owner_ref[:, at]
            kept = back[:, at]
            for k in range(GROUP):
                kept = kept + jnp.where(owners == names[k], prod[k * chan:(k + 1) * chan], 0.0)
            back[:, at] = kept
        return carry

    lax.fori_loop(0, peers // GROUP, collect, 0)

    for n, source in enumerate((up, down, far)):
        shared(source).wait_recv()
        share(4 + n, source, sibling).start()

    step = min(256, fold)

    def scatter(values, where):
        n = where.shape[1]
        high, low = where >> per, where & (fold - 1)
        for g in range(FOLD):
            spread[g * chan:(g + 1) * chan, :] = values * hot(high == g)
        for r in range(fold // step):
            here = hot(iota((step, n), 0) + r * step == low)
            acc[:, r * step:(r + 1) * step] += lax.dot_general(
                spread[...], here, NT, preferred_element_type=F32)

    width = BATCH * cap

    def add_back(b, carry):
        at = pl.ds(pl.multiple_of(b * width, width), width)
        factor = score_ref[:, at] * (1.0 / math.sqrt(C))
        scatter((back[:, at] * factor).astype(BF), donor_ref[:, at])
        return carry

    lax.fori_loop(0, count // width, add_back, 0)

    def add_terms(group, carry):
        values, where = [], []
        for k in range(BATCH):
            other = lax.rem(me + peers - (group * BATCH + k), peers)

            @pl.when(other != me)
            def _():
                arrival(1, other).wait_recv()
            values.append(terms_in[other])
            where.append(rows_in[other])
        scatter(jnp.concatenate(values, axis=1), jnp.concatenate(where, axis=1))
        return carry

    lax.fori_loop(0, peers // BATCH, add_terms, 0)

    pair = min(256, fold)
    half_pair = pair // 2
    goal = iota((pair, pair), 1)
    pick = hot(iota((pair, pair), 0) == jnp.where(goal < half_pair, 2 * goal, 2 * (goal - half_pair) + 1))
    edge = halo_even.shape[1]
    to_up = pltpu.make_async_remote_copy(
        taps.at[pl.ds(2 * chan, chan), pl.ds(wide - edge, edge)], halo_odd, halo_send.at[0], halo_recv.at[0],
        device_id={"pos": lax.rem(me + 1, peers)}, device_id_type=MESH)
    to_down = pltpu.make_async_remote_copy(
        taps.at[pl.ds(chan, chan), pl.ds(0, edge)], halo_even, halo_send.at[1], halo_recv.at[1],
        device_id={"pos": lax.rem(me + peers - 1, peers)}, device_id_type=MESH)
    last_q = fold // pair - 1
    for q in [0, last_q] + list(range(1, last_q)):
        at = slice(q * pair, (q + 1) * pair)
        skip = acc[:, at].astype(BF)
        split = jnp.dot(skip, pick, preferred_element_type=F32).astype(BF)
        for g in range(FOLD):
            rows_of = slice(g * chan, (g + 1) * chan)
            skip_ref[:, g * fold + q * pair:g * fold + (q + 1) * pair] = skip[rows_of]
            start = (g * fold + q * pair) // 2
            taps[chan:2 * chan, start:start + half_pair] = split[rows_of, :half_pair]
            taps[2 * chan:3 * chan, start:start + half_pair] = split[rows_of, half_pair:]
        if q == last_q:
            to_down.start()
            to_up.start()
    spot = iota((chan, wide), 1)
    taps[0:chan, :] = pltpu.roll(taps[2 * chan:3 * chan, :].astype(F32), 1, 1).astype(BF)
    taps[3 * chan:4 * chan, :] = pltpu.roll(taps[chan:2 * chan, :].astype(F32), wide - 1, 1).astype(BF)

    half = ring * chan

    def pair_copy(q):
        return pltpu.make_async_remote_copy(
            pair_out.at[q], pair_in.at[q], pair_send.at[q], pair_recv.at[q],
            device_id={"ch": sibling}, device_id_type=MESH)

    def relay_copy(q):
        return pltpu.make_async_remote_copy(
            part.at[q, row_far], relay.at[q], relay_send.at[q], relay_recv.at[q],
            device_id={"ch": up if q < PARTS // 2 else down}, device_id_type=MESH)

    def direct_copy(q):
        rising = q >= PARTS // 2
        return pltpu.make_async_remote_copy(
            part.at[q, row_up if rising else row_down], (before if rising else after).at[q],
            direct_send.at[q], direct_recv.at[q],
            device_id={"ch": up if rising else down}, device_id_type=MESH)

    def sum_copy(q):
        rising = q < PARTS // 2
        return pltpu.make_async_remote_copy(
            part.at[q, row_up if rising else row_down], (before if rising else after).at[q],
            sum_send.at[q], sum_recv.at[q],
            device_id={"ch": up if rising else down}, device_id_type=MESH)

    def columns(q):
        return slice(q * piece, (q + 1) * piece)

    def for_sibling(q):
        pair_out[q] = jnp.dot(
            wt[pl.ds(pl.multiple_of((1 - core) * half, half), half), :], taps[:, columns(q)], preferred_element_type=F32
        ).astype(BF).reshape(ring, chan, piece)
        pair_copy(q).start()

    def for_ring(q):
        mine = jnp.dot(
            wt[pl.ds(pl.multiple_of(core * half, half), half), :], taps[:, columns(q)], preferred_element_type=F32)
        pair_copy(q).wait_recv()
        both = mine.reshape(ring, chan, piece) + pair_in[q].astype(F32)
        exact[q] = both
        part[q] = both.astype(BF)
        relay_copy(q).start()

    order = (1, 2, 0, 3)
    for_sibling(1)
    for_sibling(2)
    for_ring(1)
    to_up.wait()
    to_down.wait()
    first = halo_odd[...].astype(F32)[:, edge - 1:edge] * jnp.where(me == 0, 0.0, 1.0)
    last = halo_even[...].astype(F32)[:, 0:1] * jnp.where(me == peers - 1, 0.0, 1.0)
    lane = iota((chan, edge), 1)
    taps[0:chan, 0:edge] = jnp.where(lane == 0, first, taps[0:chan, 0:edge].astype(F32)).astype(BF)
    taps[3 * chan:4 * chan, wide - edge:wide] = jnp.where(
        lane == edge - 1, last, taps[3 * chan:4 * chan, wide - edge:wide].astype(F32)).astype(BF)
    for_sibling(0)
    for_ring(2)
    for_sibling(3)
    for_ring(0)
    for_ring(3)
    for q in order:
        direct_copy(q).start()

    load_coarse.wait()
    for source in (sibling, lax.rem(sibling + 2, 2 * ring), lax.rem(sibling + 4, 2 * ring), lax.rem(sibling + 6, 2 * ring)):
        shared(source).wait_recv()
    for q in range(PARTS):
        term = lax.dot_general(full[:, columns(q)], taps[:, columns(q)], NT, preferred_element_type=F32)
        if q == 0:
            weight_acc[...] = term
        else:
            weight_acc[...] += term
    group_rows = channels // outer
    for x in range(outer):
        first_out[x] = weight_acc[x * group_rows:(x + 1) * group_rows, :].astype(BF)

    def first_copy(off):
        other = lax.rem(mine_out + off, outer)
        return pltpu.make_async_remote_copy(
            first_out.at[other], first_in.at[mine_out], first_send.at[other], first_recv.at[mine_out],
            device_id={"pos": other * inner + mine_in}, device_id_type=MESH)

    def first_arrival(off):
        source = lax.rem(mine_out + off, outer)
        return pltpu.make_async_remote_copy(
            first_out.at[source], first_in.at[source], first_send.at[source], first_recv.at[source],
            device_id={"pos": source * inner + mine_in}, device_id_type=MESH), source

    def second_copy(off):
        other = lax.rem(mine_in + off, inner)
        return pltpu.make_async_remote_copy(
            second_out.at[other], second_in.at[mine_in], second_send.at[other], second_recv.at[mine_in],
            device_id={"pos": mine_out * inner + other}, device_id_type=MESH)

    def second_arrival(off):
        source = lax.rem(mine_in + off, inner)
        return pltpu.make_async_remote_copy(
            second_out.at[source], second_in.at[source], second_send.at[source], second_recv.at[source],
            device_id={"pos": mine_out * inner + source}, device_id_type=MESH), source

    for off in range(1, outer):
        first_copy(off).start()

    def pass_on(q):
        rising = q < PARTS // 2
        relay_copy(q).wait_recv()
        to = row_up if rising else row_down
        part[q, to] = (exact[q, to] + relay[q].astype(F32)).astype(BF)
        sum_copy(q).start()

    pass_on(order[0])
    pass_on(order[1])

    partial = weight_acc[pl.ds(pl.multiple_of(mine_out * group_rows, group_rows), group_rows), :]
    for off in range(1, outer):
        came, source = first_arrival(off)
        came.wait_recv()
        partial = partial + first_in[source].astype(F32)
    kept = second_out.shape[1]
    blank = jnp.zeros((kept - rows_each, partial.shape[1]), F32)
    for z in range(inner):
        second_out[z] = jnp.concatenate([partial[z * rows_each:(z + 1) * rows_each], blank], axis=0).astype(BF)
    for off in range(1, inner):
        second_copy(off).start()

    pass_on(order[2])
    pass_on(order[3])

    done = second_out[mine_in].astype(F32)
    for off in range(1, inner):
        came, source = second_arrival(off)
        came.wait_recv()
        done = done + second_in[source].astype(F32)
    done = done * (1.0 / math.sqrt(total))
    fill = jnp.zeros((128 - kept, done.shape[1]), F32)
    turned = jnp.concatenate([done, fill], axis=0).T[:, 0:rows_each]
    for k in range(KERNEL):
        weight_ref[k] = turned[k * chan:(k + 1) * chan].astype(BF)

    for q in order:
        direct_copy(q).wait_recv()
        sum_copy(q).wait_recv()
        coarse_ref[:, columns(q)] = (exact[q, row] + before[q].astype(F32) + after[q].astype(F32)).astype(BF)

    for n, to in enumerate((up, down, far, sibling)):
        share(n, ch, to).wait_send()
    for n, source in enumerate((up, down, far)):
        share(4 + n, source, sibling).wait_send()

    def drain(off):
        other = lax.rem(me + off, peers)
        for kind in range(3):
            send(kind, other).wait_send()

    each(1, drain)
    for q in order:
        pair_copy(q).wait_send()
        relay_copy(q).wait_send()
        direct_copy(q).wait_send()
        sum_copy(q).wait_send()
    for off in range(1, outer):
        first_copy(off).wait_send()
    for off in range(1, inner):
        second_copy(off).wait_send()


def section(track_grad, activation, coarse_in, tap_weight, score_grad, donor_row, owner, acceptor_row, peers, ring):
    chan, length = activation.shape
    wide = coarse_in.shape[1]
    channels = tap_weight.shape[2]
    count = owner.shape[1]
    cap = count // 8
    fold = length // FOLD
    piece = wide // PARTS
    inner = min(8, peers // 2)
    outer = peers // inner
    outs = KERNEL * chan
    rows_each = channels // peers
    kept = -(-rows_each // 16) * 16
    edge = min(128, wide)
    dma = pltpu.SemaphoreType.DMA
    vmem = pl.BlockSpec(memory_space=pltpu.VMEM)
    hbm = pl.BlockSpec(memory_space=pl.ANY)
    slots = pltpu.VMEM((peers, chan, cap), BF)
    names = pltpu.VMEM((peers, 1, cap), jnp.int32)
    quarter = pltpu.VMEM((PARTS, ring, chan, piece), BF)
    eighth = pltpu.VMEM((PARTS, chan, piece), BF)
    return pl.pallas_call(
        functools.partial(section_kernel, peers, inner, ring, wide * peers),
        out_shape=(
            jax.ShapeDtypeStruct((chan, length), BF),
            jax.ShapeDtypeStruct((chan, wide), BF),
            jax.ShapeDtypeStruct((KERNEL, chan, rows_each), BF),
        ),
        in_specs=[hbm, hbm, hbm, vmem, vmem, vmem, vmem, vmem],
        out_specs=(vmem, vmem, vmem),
        scratch_shapes=[
            pltpu.VMEM((FOLD * chan, fold), BF),
            pltpu.VMEM((FOLD * chan, fold), BF),
            pltpu.VMEM((FOLD * chan, fold), F32),
            pltpu.VMEM((cap, count), BF),
            pltpu.VMEM((chan, count), BF),
            pltpu.VMEM((GROUP * chan, count), BF),
            pltpu.VMEM((FOLD * chan, BATCH * cap), BF),
            pltpu.VMEM((chan, count), F32),
            names, names, slots, slots, slots, slots,
            pltpu.VMEM((channels, wide), BF),
            pltpu.VMEM((channels, outs), BF),
            pltpu.VMEM((outs, wide), BF),
            pltpu.VMEM((chan, edge), BF),
            pltpu.VMEM((chan, edge), BF),
            quarter, quarter, quarter,
            pltpu.VMEM((PARTS, ring, chan, piece), F32),
            eighth, eighth, eighth,
            pltpu.VMEM((channels, outs), F32),
            pltpu.VMEM((outer, channels // outer, outs), BF),
            pltpu.VMEM((outer, channels // outer, outs), BF),
            pltpu.VMEM((inner, kept, outs), BF),
            pltpu.VMEM((inner, kept, outs), BF),
            dma((3, FOLD)),
            dma((peers,)), dma((peers,)), dma((peers,)), dma((peers,)), dma((peers,)), dma((peers,)),
            dma((7,)), dma((2 * ring,)), dma((2,)), dma((2,)),
            dma((PARTS,)), dma((PARTS,)), dma((PARTS,)), dma((PARTS,)),
            dma((PARTS,)), dma((PARTS,)), dma((PARTS,)), dma((PARTS,)),
            dma((outer,)), dma((outer,)), dma((inner,)), dma((inner,)),
        ],
        compiler_params=pltpu.CompilerParams(
            collective_id=1, has_side_effects=True, vmem_limit_bytes=60 * 1024 * 1024),
        name="section",
    )(activation, track_grad, coarse_in, tap_weight, owner, acceptor_row, donor_row, score_grad)


def shards(
    track_grad,
    activation,
    coarse_in,
    tap_weight,
    score_grad,
    donor_row,
    acceptor_owner,
    acceptor_row,
):
    return section(
        track_grad,
        activation,
        coarse_in,
        tap_weight,
        score_grad.reshape(1, -1),
        donor_row.reshape(1, -1),
        acceptor_owner.reshape(1, -1),
        acceptor_row.reshape(1, -1),
        lax.axis_size("pos"),
        lax.axis_size("ch") // 2,
    )


def solution(mesh):
    in_specs = (
        P("ch", "pos"),
        P("ch", "pos"),
        P("ch", "pos"),
        P(None, "ch", None),
        P("pos"),
        P("pos"),
        P("pos", None),
        P("pos"),
    )
    out_specs = (P("ch", "pos"), P("ch", "pos"), P(None, "ch", "pos"))
    return jax.shard_map(shards, mesh=mesh, in_specs=in_specs, out_specs=out_specs, check_vma=False)
```

time: 610 us -> 136 us (0.22)
  waiting for transfers between devices: 230 us -> 0 us
  local copies, waits for them, and re-layouts: 199 us -> 5.19 us
  Pallas kernels: 0 us -> 130 us
  other arithmetic: 115 us -> 0 us
  starting transfers between devices: 35 us -> 0 us
  matrix products: 15.7 us -> 0 us
  between operations: 14.7 us -> 0.64 us
    unnamed x5 -> x0, waiting for transfers between devices: 202 us -> none
    pallas_call x0 -> x1, Pallas kernels: none -> 130 us  [section(): pl.pallas_call(functools.partial(section_kernel, peers, inner, ring, wide...]
    slice x6 -> x0, local copies, waits for them, and re-layouts: 112 us -> none  [the longest x4 112 us: shards(): extended[:, offset:offset + local_len:2]]
    scatter-add x2 -> x0, other arithmetic: 84.6 us -> none  [the longest x1 59.1 us: shards(): running.at[:, got_rows.reshape(-1)]]
    gather x2 -> x0, local copies, waits for them, and re-layouts: 32.5 us -> none  [shards(): fetched = jnp.take(activation, got_rows[0], axis=1)]
    all_to_all x3 -> x0, starting transfers between devices: 29 us -> none  [the longest x1 11.9 us: shards(): lax.all_to_all(request_rows, 'pos', split_axis=1, concat_axis=1, tiled=True)]
    all_to_all x3 -> x0, waiting for transfers between devices: 27.7 us -> none  [the longest x1 24.8 us: shards(): lax.all_to_all(fetched, 'pos', split_axis=1, concat_axis=1, tiled=True)]
    unnamed x20 -> x4, local copies, waits for them, and re-layouts: 20.7 us -> 3.61 us
  transfers between devices with their start and end apart: 8 -> 0, of which waited for: 4 -> 0; matrix products, arithmetic and copies ran while one was open for 52% -> 0% of each run, Pallas kernels for 0% -> 0%
where the time goes in v3:
time: 136 us
  Pallas kernels  130 us (96%)
  local copies, waits for them, and re-layouts  5.19 us (4%)
    pallas_call x1, Pallas kernels, section(): pl.pallas_call(functools.partial(section_kernel, peers, inner, ring, wide...  130 us
    unnamed x4, local copies, waits for them, and re-layouts  3.61 us

profile of v3, /device:TPU:1, one launch (start us, length us, event | category | flops | bytes accessed | tf_op | source)
XLA Modules:
  0.0 135.8 jit_solution(11699534067264871114)
XLA Ops:
  0.6 130.0 %section.1 = (bf16[96,8192]{1,0:T(8,128)(2,1)}, bf16[96,4096]{1,0:T(8,128)(2,1)}, bf16[4,96,24]{2,1,0:T(8,128)(2,1)}) custom-call(bf16[96,8192]{1,0:T(8,128)(2,1)} %act_hbm.1, bf16[96,8192]{1,0:T(8,128)(2,1)} %track_hbm.1, bf16[96,4096]{1,0:T(8,128)(2,1)} %coarse_hbm.1, bf16[4,96,768]{2,1,0:T(8,128)(2,1)} %weight_in_ref.1, s32[1,2048]{1,0:T(1,128)} %bitcast.4, ...), custom_call_target="tpu_custom_call" | custom-call | tf_op jit(solution)/shard_map/section/pallas_call | solution.py:483
  130.6 1.6 %copy.11 = bf16[4,96,24]{1,2,0:T(8,128)(2,1)} copy(bf16[4,96,24]{2,1,0:T(8,128)(2,1)} %get-tuple-element.5) | data formatting | bytes 36864 | tf_op jit(solution)/shard_map/section/pallas_call | solution.py:483
  132.2 0.0 copy-start
  132.2 2.7 %copy.14 = bf16[96,8192]{1,0:T(8,128)(2,1)} copy(bf16[96,8192]{1,0:T(8,128)(2,1)} %get-tuple-element.9) | data formatting | bytes 3145728
  134.9 0.0 copy-done
  135.0 0.9 copy.15
Async XLA Ops:
  132.2 2.7 %copy-start = (bf16[96,4096]{1,0:T(8,128)(2,1)S(1)}, bf16[96,4096]{1,0:T(8,128)(2,1)}, u32[]{:S(2)}) copy-start(bf16[96,4096]{1,0:T(8,128)(2,1)} %get-tuple-element.10) | copy-start | bytes 2359300

commit v4 on v3

--- a/solution.py
+++ b/solution.py
@@ -11,7 +11,7 @@
 C = 768
 KERNEL = 4
 FOLD = 8
-PARTS = 4
+PARTS = 8
 GROUP = 8
 BATCH = 4
 BF = jnp.bfloat16
@@ -31,14 +31,14 @@
 def section_kernel(
     peers, inner, ring, total,
     act_hbm, track_hbm, coarse_hbm, weight_in_ref, owner_ref, acceptor_ref, donor_ref, score_ref,
-    skip_ref, coarse_ref, weight_ref,
-    act, track, acc, within_hot, terms, stack, spread, back,
+    skip_hbm, out_hbm, weight_ref,
+    skip_ref, coarse_ref, act, track, acc, within_hot, terms, stack, spread, back,
     rows_out, rows_in, terms_out, terms_in, fetch_out, fetch_in,
     full, wt, taps, halo_even, halo_odd, pair_out, pair_in, part, exact, relay, before, after,
     weight_acc, first_out, first_in, second_out, second_in,
     load_sem, rows_send, rows_recv, terms_send, terms_recv, fetch_send, fetch_recv,
     gather_send, gather_recv, halo_send, halo_recv, pair_send, pair_recv, relay_send, relay_recv,
-    direct_send, direct_recv, sum_send, sum_recv, first_send, first_recv, second_send, second_recv,
+    direct_send, direct_recv, sum_send, sum_recv, first_send, first_recv, second_send, second_recv, store_sem,
 ):
     me = lax.axis_index("pos")
     ch = lax.axis_index("ch")
@@ -105,43 +105,6 @@
         rows_out[p] = rows[p:p + 1, :]
     rows_in[me] = rows_out[me]
 
-    pl.semaphore_wait(barrier, peers + 3)
-
-    kinds = (
-        (rows_out, rows_in, rows_send, rows_recv),
-        (terms_out, terms_in, terms_send, terms_recv),
-        (fetch_out, fetch_in, fetch_send, fetch_recv),
-    )
-
-    def send(kind, other):
-        out, into, sent, got = kinds[kind]
-        return pltpu.make_async_remote_copy(
-            out.at[other], into.at[me], sent.at[other], got.at[me],
-            device_id={"pos": other}, device_id_type=MESH)
-
-    def arrival(kind, other):
-        out, into, sent, got = kinds[kind]
-        return pltpu.make_async_remote_copy(
-            out.at[other], into.at[other], sent.at[other], got.at[other],
-            device_id={"pos": other}, device_id_type=MESH)
-
-    each(1, lambda off: send(0, lax.rem(me + off, peers)).start())
-
-    def share(n, source, goal):
-        span = pl.ds(pl.multiple_of(source * chan, chan), chan)
-        return pltpu.make_async_remote_copy(
-            coarse_hbm if n < 4 else full.at[span, :], full.at[span, :], gather_send.at[n], gather_recv.at[source],
-            device_id={"ch": goal}, device_id_type=MESH)
-
-    for n, goal in enumerate((up, down, far, sibling)):
-        share(n, ch, goal).start()
-
-    def shared(source):
-        span = pl.ds(pl.multiple_of(source * chan, chan), chan)
-        return pltpu.make_async_remote_copy(
-            full.at[span, :], full.at[span, :], gather_send.at[0], gather_recv.at[source],
-            device_id={"ch": sibling}, device_id_type=MESH)
-
     def gather(where):
         spot = iota((fold, where.shape[1]), 0)
         prod = jnp.dot(act[...], hot(spot == (where & (fold - 1))), preferred_element_type=F32)
@@ -162,16 +125,7 @@
 
     lax.fori_loop(0, blocks, make_terms, 0)
 
-    def answer(off):
-        other = lax.rem(me + off, peers)
-        arrival(0, other).wait_recv()
-        fetch_out[other] = gather(rows_in[other]).astype(BF)
-        send(2, other).start()
-
-    each(1, answer)
-    fetch_in[me] = gather(rows_in[me]).astype(BF)
-
-    def expand(group, carry):
+    def expand(group):
         for k in range(GROUP):
             other = lax.rem(me + group * GROUP + k, peers)
             stack[k * chan:(k + 1) * chan, :] = terms[...] * hot(owner_ref[...] == other)
@@ -180,13 +134,67 @@
             other = lax.rem(me + group * GROUP + k, peers)
             terms_out[other] = slotted[k * chan:(k + 1) * chan, :].astype(BF)
 
-            @pl.when(other != me)
-            def _():
-                send(1, other).start()
+    def leave(group, first):
+        for k in range(first, GROUP):
+            send(1, lax.rem(me + group * GROUP + k, peers)).start()
+
+    def expand_next(group, carry):
+        expand(group)
+        leave(group, 0)
         return carry
 
-    lax.fori_loop(0, peers // GROUP, expand, 0)
+    expand(0)
     terms_in[me] = terms_out[me]
+
+    pl.semaphore_wait(barrier, peers + 3)
+
+    kinds = (
+        (rows_out, rows_in, rows_send, rows_recv),
+        (terms_out, terms_in, terms_send, terms_recv),
+        (fetch_out, fetch_in, fetch_send, fetch_recv),
+    )
+
+    def send(kind, other):
+        out, into, sent, got = kinds[kind]
+        return pltpu.make_async_remote_copy(
+            out.at[other], into.at[me], sent.at[other], got.at[me],
+            device_id={"pos": other}, device_id_type=MESH)
+
+    def arrival(kind, other):
+        out, into, sent, got = kinds[kind]
+        return pltpu.make_async_remote_copy(
+            out.at[other], into.at[other], sent.at[other], got.at[other],
+            device_id={"pos": other}, device_id_type=MESH)
+
+    each(1, lambda off: send(0, lax.rem(me + off, peers)).start())
+
+    leave(0, 1)
+
+    def share(n, source, goal):
+        span = pl.ds(pl.multiple_of(source * chan, chan), chan)
+        return pltpu.make_async_remote_copy(
+            coarse_hbm if n < 4 else full.at[span, :], full.at[span, :], gather_send.at[n], gather_recv.at[source],
+            device_id={"ch": goal}, device_id_type=MESH)
+
+    for n, goal in enumerate((up, down, far, sibling)):
+        share(n, ch, goal).start()
+
+    def shared(source):
+        span = pl.ds(pl.multiple_of(source * chan, chan), chan)
+        return pltpu.make_async_remote_copy(
+            full.at[span, :], full.at[span, :], gather_send.at[0], gather_recv.at[source],
+            device_id={"ch": sibling}, device_id_type=MESH)
+
+    def answer(off):
+        other = lax.rem(me + off, peers)
+        arrival(0, other).wait_recv()
+        fetch_out[other] = gather(rows_in[other]).astype(BF)
+        send(2, other).start()
+
+    each(1, answer)
+    fetch_in[me] = gather(rows_in[me]).astype(BF)
+
+    lax.fori_loop(1, peers // GROUP, expand_next, 0)
 
     for g in range(FOLD):
         load(1, track_hbm, track, g).wait()
@@ -232,11 +240,11 @@
         n = where.shape[1]
         high, low = where >> per, where & (fold - 1)
         for g in range(FOLD):
-            spread[g * chan:(g + 1) * chan, :] = values * hot(high == g)
+            spread[g * chan:(g + 1) * chan, 0:n] = values * hot(high == g)
         for r in range(fold // step):
             here = hot(iota((step, n), 0) + r * step == low)
             acc[:, r * step:(r + 1) * step] += lax.dot_general(
-                spread[...], here, NT, preferred_element_type=F32)
+                spread[:, 0:n], here, NT, preferred_element_type=F32)
 
     width = BATCH * cap
 
@@ -248,10 +256,10 @@
 
     lax.fori_loop(0, count // width, add_back, 0)
 
-    def add_terms(group, carry):
+    def add_terms(start, size):
         values, where = [], []
-        for k in range(BATCH):
-            other = lax.rem(me + peers - (group * BATCH + k), peers)
+        for k in range(size):
+            other = lax.rem(me + 2 * peers - (start + k), peers)
 
             @pl.when(other != me)
             def _():
@@ -259,9 +267,14 @@
             values.append(terms_in[other])
             where.append(rows_in[other])
         scatter(jnp.concatenate(values, axis=1), jnp.concatenate(where, axis=1))
+
+    def add_batch(group, carry):
+        add_terms(group * BATCH, BATCH)
         return carry
 
-    lax.fori_loop(0, peers // BATCH, add_terms, 0)
+    lax.fori_loop(0, peers // BATCH - 1, add_batch, 0)
+    add_terms(peers - BATCH, BATCH // 2)
+    add_terms(peers - BATCH // 2, BATCH // 2)
 
     pair = min(256, fold)
     half_pair = pair // 2
@@ -288,7 +301,8 @@
         if q == last_q:
             to_down.start()
             to_up.start()
-    spot = iota((chan, wide), 1)
+    store_skip = pltpu.make_async_copy(skip_ref, skip_hbm, store_sem.at[0])
+    store_skip.start()
     taps[0:chan, :] = pltpu.roll(taps[2 * chan:3 * chan, :].astype(F32), 1, 1).astype(BF)
     taps[3 * chan:4 * chan, :] = pltpu.roll(taps[chan:2 * chan, :].astype(F32), wide - 1, 1).astype(BF)
 
@@ -336,31 +350,33 @@
         part[q] = both.astype(BF)
         relay_copy(q).start()
 
-    order = (1, 2, 0, 3)
-    for_sibling(1)
-    for_sibling(2)
-    for_ring(1)
-    to_up.wait()
-    to_down.wait()
-    first = halo_odd[...].astype(F32)[:, edge - 1:edge] * jnp.where(me == 0, 0.0, 1.0)
-    last = halo_even[...].astype(F32)[:, 0:1] * jnp.where(me == peers - 1, 0.0, 1.0)
-    lane = iota((chan, edge), 1)
-    taps[0:chan, 0:edge] = jnp.where(lane == 0, first, taps[0:chan, 0:edge].astype(F32)).astype(BF)
-    taps[3 * chan:4 * chan, wide - edge:wide] = jnp.where(
-        lane == edge - 1, last, taps[3 * chan:4 * chan, wide - edge:wide].astype(F32)).astype(BF)
-    for_sibling(0)
-    for_ring(2)
-    for_sibling(3)
-    for_ring(0)
-    for_ring(3)
+    low = list(range(1, PARTS // 2)) + [0]
+    order = [q for both in zip(low, range(PARTS // 2, PARTS)) for q in both]
+    for_sibling(order[0])
+    for_sibling(order[1])
+    for n in range(PARTS):
+        for_ring(order[n])
+        if n + 2 == PARTS - 2:
+            to_up.wait()
+            to_down.wait()
+            first = halo_odd[...].astype(F32)[:, edge - 1:edge] * jnp.where(me == 0, 0.0, 1.0)
+            last = halo_even[...].astype(F32)[:, 0:1] * jnp.where(me == peers - 1, 0.0, 1.0)
+            lane = iota((chan, edge), 1)
+            taps[0:chan, 0:edge] = jnp.where(lane == 0, first, taps[0:chan, 0:edge].astype(F32)).astype(BF)
+            taps[3 * chan:4 * chan, wide - edge:wide] = jnp.where(
+                lane == edge - 1, last, taps[3 * chan:4 * chan, wide - edge:wide].astype(F32)).astype(BF)
+        if n + 2 < PARTS:
+            for_sibling(order[n + 2])
     for q in order:
         direct_copy(q).start()
 
     load_coarse.wait()
     for source in (sibling, lax.rem(sibling + 2, 2 * ring), lax.rem(sibling + 4, 2 * ring), lax.rem(sibling + 6, 2 * ring)):
         shared(source).wait_recv()
-    for q in range(PARTS):
-        term = lax.dot_general(full[:, columns(q)], taps[:, columns(q)], NT, preferred_element_type=F32)
+    quarter = wide // 4
+    for q in range(4):
+        span = slice(q * quarter, (q + 1) * quarter)
+        term = lax.dot_general(full[:, span], taps[:, span], NT, preferred_element_type=F32)
         if q == 0:
             weight_acc[...] = term
         else:
@@ -403,58 +419,62 @@
         part[q, to] = (exact[q, to] + relay[q].astype(F32)).astype(BF)
         sum_copy(q).start()
 
-    pass_on(order[0])
-    pass_on(order[1])
+    def drain(off):
+        other = lax.rem(me + off, peers)
+        for kind in range(3):
+            send(kind, other).wait_send()
+
+    each(1, drain)
+
+    for q in order[:PARTS // 2]:
+        pass_on(q)
 
     partial = weight_acc[pl.ds(pl.multiple_of(mine_out * group_rows, group_rows), group_rows), :]
     for off in range(1, outer):
         came, source = first_arrival(off)
         came.wait_recv()
         partial = partial + first_in[source].astype(F32)
-    kept = second_out.shape[1]
-    blank = jnp.zeros((kept - rows_each, partial.shape[1]), F32)
     for z in range(inner):
-        second_out[z] = jnp.concatenate([partial[z * rows_each:(z + 1) * rows_each], blank], axis=0).astype(BF)
+        second_out[z] = partial[z * rows_each:(z + 1) * rows_each]
     for off in range(1, inner):
         second_copy(off).start()
 
-    pass_on(order[2])
-    pass_on(order[3])
-
-    done = second_out[mine_in].astype(F32)
+    for q in order[PARTS // 2:]:
+        pass_on(q)
+
+    for n, to in enumerate((up, down, far, sibling)):
+        share(n, ch, to).wait_send()
+    for n, source in enumerate((up, down, far)):
+        share(4 + n, source, sibling).wait_send()
+    store_skip.wait()
+    for q in order:
+        pair_copy(q).wait_send()
+        relay_copy(q).wait_send()
+    for off in range(1, outer):
+        first_copy(off).wait_send()
+
+    done = second_out[mine_in]
     for off in range(1, inner):
         came, source = second_arrival(off)
         came.wait_recv()
-        done = done + second_in[source].astype(F32)
+        done = done + second_in[source]
     done = done * (1.0 / math.sqrt(total))
-    fill = jnp.zeros((128 - kept, done.shape[1]), F32)
-    turned = jnp.concatenate([done, fill], axis=0).T[:, 0:rows_each]
     for k in range(KERNEL):
-        weight_ref[k] = turned[k * chan:(k + 1) * chan].astype(BF)
+        weight_ref[k] = done[:, k * chan:(k + 1) * chan].astype(BF)
+
+    def store(q):
+        return pltpu.make_async_copy(coarse_ref.at[:, columns(q)], out_hbm.at[:, columns(q)], store_sem.at[1 + q])
 
     for q in order:
         direct_copy(q).wait_recv()
         sum_copy(q).wait_recv()
         coarse_ref[:, columns(q)] = (exact[q, row] + before[q].astype(F32) + after[q].astype(F32)).astype(BF)
-
-    for n, to in enumerate((up, down, far, sibling)):
-        share(n, ch, to).wait_send()
-    for n, source in enumerate((up, down, far)):
-        share(4 + n, source, sibling).wait_send()
-
-    def drain(off):
-        other = lax.rem(me + off, peers)
-        for kind in range(3):
-            send(kind, other).wait_send()
-
-    each(1, drain)
+        store(q).start()
+
     for q in order:
-        pair_copy(q).wait_send()
-        relay_copy(q).wait_send()
         direct_copy(q).wait_send()
         sum_copy(q).wait_send()
-    for off in range(1, outer):
-        first_copy(off).wait_send()
+        store(q).wait()
     for off in range(1, inner):
         second_copy(off).wait_send()
 
@@ -471,7 +491,6 @@
     outer = peers // inner
     outs = KERNEL * chan
     rows_each = channels // peers
-    kept = -(-rows_each // 16) * 16
     edge = min(128, wide)
     dma = pltpu.SemaphoreType.DMA
     vmem = pl.BlockSpec(memory_space=pltpu.VMEM)
@@ -485,11 +504,13 @@
         out_shape=(
             jax.ShapeDtypeStruct((chan, length), BF),
             jax.ShapeDtypeStruct((chan, wide), BF),
-            jax.ShapeDtypeStruct((KERNEL, chan, rows_each), BF),
+            jax.ShapeDtypeStruct((KERNEL, rows_each, chan), BF),
         ),
         in_specs=[hbm, hbm, hbm, vmem, vmem, vmem, vmem, vmem],
-        out_specs=(vmem, vmem, vmem),
+        out_specs=(hbm, hbm, vmem),
         scratch_shapes=[
+            pltpu.VMEM((chan, length), BF),
+            pltpu.VMEM((chan, wide), BF),
             pltpu.VMEM((FOLD * chan, fold), BF),
             pltpu.VMEM((FOLD * chan, fold), BF),
             pltpu.VMEM((FOLD * chan, fold), F32),
@@ -510,19 +531,50 @@
             pltpu.VMEM((channels, outs), F32),
             pltpu.VMEM((outer, channels // outer, outs), BF),
             pltpu.VMEM((outer, channels // outer, outs), BF),
-            pltpu.VMEM((inner, kept, outs), BF),
-            pltpu.VMEM((inner, kept, outs), BF),
+            pltpu.VMEM((inner, rows_each, outs), F32),
+            pltpu.VMEM((inner, rows_each, outs), F32),
             dma((3, FOLD)),
             dma((peers,)), dma((peers,)), dma((peers,)), dma((peers,)), dma((peers,)), dma((peers,)),
             dma((7,)), dma((2 * ring,)), dma((2,)), dma((2,)),
             dma((PARTS,)), dma((PARTS,)), dma((PARTS,)), dma((PARTS,)),
             dma((PARTS,)), dma((PARTS,)), dma((PARTS,)), dma((PARTS,)),
-            dma((outer,)), dma((outer,)), dma((inner,)), dma((inner,)),
+            dma((outer,)), dma((outer,)), dma((inner,)), dma((inner,)), dma((1 + PARTS,)),
         ],
         compiler_params=pltpu.CompilerParams(
             collective_id=1, has_side_effects=True, vmem_limit_bytes=60 * 1024 * 1024),
         name="section",
     )(activation, track_grad, coarse_in, tap_weight, owner, acceptor_row, donor_row, score_grad)
+
+
+def deliver_kernel(skip_in, coarse_in, weight_in, skip_out, coarse_out, weight_out, skip, coarse, weight, sem):
+    parts = 6
+    rows = skip.shape[0] // parts
+    moves = [(weight_in, weight, weight_out)]
+    for n in range(parts):
+        span = pl.ds(n * rows, rows)
+        for source, held, goal in ((skip_in, skip, skip_out), (coarse_in, coarse, coarse_out)):
+            moves.append((source.at[span, :], held.at[span, :], goal.at[span, :]))
+    into = [pltpu.make_async_copy(a, b, sem.at[0, n]) for n, (a, b, _) in enumerate(moves)]
+    out = [pltpu.make_async_copy(b, c, sem.at[1, n]) for n, (_, b, c) in enumerate(moves)]
+    for copy in into:
+        copy.start()
+    for first, second in zip(into, out):
+        first.wait()
+        second.start()
+    for copy in out:
+        copy.wait()
+
+
+def deliver(*arrays):
+    hbm = pl.BlockSpec(memory_space=pl.ANY)
+    return pl.pallas_call(
+        deliver_kernel,
+        out_shape=tuple(jax.ShapeDtypeStruct(a.shape, a.dtype) for a in arrays),
+        in_specs=[hbm] * 3,
+        out_specs=(hbm,) * 3,
+        scratch_shapes=[pltpu.VMEM(a.shape, a.dtype) for a in arrays] + [pltpu.SemaphoreType.DMA((2, 13))],
+        name="deliver",
+    )(*arrays)
 
 
 def shards(
@@ -535,7 +587,7 @@
     acceptor_owner,
     acceptor_row,
 ):
-    return section(
+    skip_grad, coarse_grad, weight_grad = section(
         track_grad,
         activation,
         coarse_in,
@@ -547,6 +599,8 @@
         lax.axis_size("pos"),
         lax.axis_size("ch") // 2,
     )
+    skip_grad, coarse_grad, weight_grad = deliver(skip_grad, coarse_grad, weight_grad)
+    return (skip_grad, coarse_grad, weight_grad.transpose(0, 2, 1))
 
 
 def solution(mesh):

time: 136 us -> 127 us (0.934)
  local copies, waits for them, and re-layouts: 5.19 us -> 0 us
  Pallas kernels: 130 us -> 126 us
    pallas_call x1, Pallas kernels: 130 us -> 124 us  [section(): pl.pallas_call(functools.partial(section_kernel, peers, inner, ring, wide...]
    unnamed x4 -> x0, local copies, waits for them, and re-layouts: 3.61 us -> none
    pallas_call x0 -> x1, Pallas kernels: none -> 2.6 us  [deliver(): pl.pallas_call(deliver_kernel, out_shape=tuple((jax.ShapeDtypeStruct(a.sh...]
    pallas_call x1 -> x0, local copies, waits for them, and re-layouts: 1.58 us -> none  [section(): pl.pallas_call(functools.partial(section_kernel, peers, inner, ring, wide...]
where the time goes in v4:
time: 127 us
  Pallas kernels  126 us (99%)
    pallas_call x1, Pallas kernels, section(): pl.pallas_call(functools.partial(section_kernel, peers, inner, ring, wide...  124 us
    pallas_call x1, Pallas kernels, deliver(): pl.pallas_call(deliver_kernel, out_shape=tuple((jax.ShapeDtypeStruct(a.sh...  2.6 us

profile of v4, /device:TPU:1, one launch (start us, length us, event | category | flops | bytes accessed | tf_op | source)
XLA Modules:
  0.0 127.0 jit_solution(10991032380401594550)
XLA Ops:
  0.6 123.6 %section.1 = (bf16[96,8192]{1,0:T(8,128)(2,1)}, bf16[96,4096]{1,0:T(8,128)(2,1)}, bf16[4,24,96]{2,1,0:T(8,128)(2,1)}) custom-call(bf16[96,8192]{1,0:T(8,128)(2,1)} %act_hbm.1, bf16[96,8192]{1,0:T(8,128)(2,1)} %track_hbm.1, bf16[96,4096]{1,0:T(8,128)(2,1)} %coarse_hbm.1, bf16[4,96,768]{2,1,0:T(8,128)(2,1)} %weight_in_ref.1, s32[1,2048]{1,0:T(1,128)} %bitcast.5, ...), custom_call_target="tpu_custom_call" | custom-call | tf_op jit(solution)/shard_map/section/pallas_call | solution.py:502
  124.3 2.6 %deliver.1 = (bf16[96,8192]{1,0:T(8,128)(2,1)}, bf16[96,4096]{1,0:T(8,128)(2,1)}, bf16[4,24,96]{2,1,0:T(8,128)(2,1)}) custom-call(bf16[96,8192]{1,0:T(8,128)(2,1)} %get-tuple-element.9.skip_in, bf16[96,4096]{1,0:T(8,128)(2,1)} %get-tuple-element.10.coarse_in, bf16[4,24,96]{2,1,0:T(8,128)(2,1)} %get-tuple-element.11.weight_in), custom_call_target="tpu_custom_call" | custom-call | tf_op jit(solution)/shard_map/deliver/pallas_call | solution.py:570

commit v5 on v4

--- a/solution.py
+++ b/solution.py
@@ -118,12 +118,12 @@
         load(0, act_hbm, act, g).wait()
 
     def make_terms(b, carry):
-        at = pl.ds(pl.multiple_of(b * cap, cap), cap)
+        at = pl.ds(pl.multiple_of(b * BATCH * cap, BATCH * cap), BATCH * cap)
         factor = score_ref[:, at] * (1.0 / math.sqrt(C))
         terms[:, at] = (gather(donor_ref[:, at]) * factor).astype(BF)
         return carry
 
-    lax.fori_loop(0, blocks, make_terms, 0)
+    lax.fori_loop(0, blocks // BATCH, make_terms, 0)
 
     def expand(group):
         for k in range(GROUP):
@@ -143,9 +143,6 @@
         leave(group, 0)
         return carry
 
-    expand(0)
-    terms_in[me] = terms_out[me]
-
     pl.semaphore_wait(barrier, peers + 3)
 
     kinds = (
@@ -167,8 +164,9 @@
             device_id={"pos": other}, device_id_type=MESH)
 
     each(1, lambda off: send(0, lax.rem(me + off, peers)).start())
-
+    expand(0)
     leave(0, 1)
+    terms_in[me] = terms_out[me]
 
     def share(n, source, goal):
         span = pl.ds(pl.multiple_of(source * chan, chan), chan)
@@ -185,15 +183,24 @@
             full.at[span, :], full.at[span, :], gather_send.at[0], gather_recv.at[source],
             device_id={"ch": sibling}, device_id_type=MESH)
 
-    def answer(off):
-        other = lax.rem(me + off, peers)
-        arrival(0, other).wait_recv()
-        fetch_out[other] = gather(rows_in[other]).astype(BF)
-        send(2, other).start()
-
-    each(1, answer)
-    fetch_in[me] = gather(rows_in[me]).astype(BF)
-
+    def look_up(first, second):
+        found = gather(jnp.concatenate([rows_in[first], rows_in[second]], axis=1)).astype(BF)
+        return found[:, :cap], found[:, cap:]
+
+    def answer(turn, carry):
+        first, second = lax.rem(me + 2 * turn + 1, peers), lax.rem(me + 2 * turn + 2, peers)
+        arrival(0, first).wait_recv()
+        arrival(0, second).wait_recv()
+        fetch_out[first], fetch_out[second] = look_up(first, second)
+        send(2, first).start()
+        send(2, second).start()
+        return carry
+
+    lax.fori_loop(0, peers // 2 - 1, answer, 0)
+    final = lax.rem(me + peers - 1, peers)
+    arrival(0, final).wait_recv()
+    fetch_out[final], fetch_in[me] = look_up(final, me)
+    send(2, final).start()
     lax.fori_loop(1, peers // GROUP, expand_next, 0)
 
     for g in range(FOLD):
@@ -206,6 +213,38 @@
                 wt[(c * ring + r) * chan:(c * ring + r + 1) * chan, k * chan:(k + 1) * chan] = (
                     turned[(2 * r + c) * chan:(2 * r + c + 1) * chan])
     back[...] = jnp.zeros_like(back)
+
+    step = min(256, fold)
+
+    def scatter(values, where):
+        n = where.shape[1]
+        high, low = where >> per, where & (fold - 1)
+        for g in range(FOLD):
+            spread[g * chan:(g + 1) * chan, 0:n] = values * hot(high == g)
+        for r in range(fold // step):
+            here = hot(iota((step, n), 0) + r * step == low)
+            acc[:, r * step:(r + 1) * step] += lax.dot_general(
+                spread[:, 0:n], here, NT, preferred_element_type=F32)
+
+    width = BATCH * cap
+
+    def add_terms(start, size):
+        values, where = [], []
+        for k in range(size):
+            other = lax.rem(me + 2 * peers - (start + k), peers)
+
+            @pl.when(other != me)
+            def _():
+                arrival(1, other).wait_recv()
+            values.append(terms_in[other])
+            where.append(rows_in[other])
+        scatter(jnp.concatenate(values, axis=1), jnp.concatenate(where, axis=1))
+
+    def add_batch(group, carry):
+        add_terms(group * BATCH, BATCH)
+        return carry
+
+    lax.fori_loop(0, GROUP // BATCH, add_batch, 0)
 
     def collect(group, carry):
         held, names = [], []
@@ -234,20 +273,6 @@
         shared(source).wait_recv()
         share(4 + n, source, sibling).start()
 
-    step = min(256, fold)
-
-    def scatter(values, where):
-        n = where.shape[1]
-        high, low = where >> per, where & (fold - 1)
-        for g in range(FOLD):
-            spread[g * chan:(g + 1) * chan, 0:n] = values * hot(high == g)
-        for r in range(fold // step):
-            here = hot(iota((step, n), 0) + r * step == low)
-            acc[:, r * step:(r + 1) * step] += lax.dot_general(
-                spread[:, 0:n], here, NT, preferred_element_type=F32)
-
-    width = BATCH * cap
-
     def add_back(b, carry):
         at = pl.ds(pl.multiple_of(b * width, width), width)
         factor = score_ref[:, at] * (1.0 / math.sqrt(C))
@@ -256,23 +281,7 @@
 
     lax.fori_loop(0, count // width, add_back, 0)
 
-    def add_terms(start, size):
-        values, where = [], []
-        for k in range(size):
-            other = lax.rem(me + 2 * peers - (start + k), peers)
-
-            @pl.when(other != me)
-            def _():
-                arrival(1, other).wait_recv()
-            values.append(terms_in[other])
-            where.append(rows_in[other])
-        scatter(jnp.concatenate(values, axis=1), jnp.concatenate(where, axis=1))
-
-    def add_batch(group, carry):
-        add_terms(group * BATCH, BATCH)
-        return carry
-
-    lax.fori_loop(0, peers // BATCH - 1, add_batch, 0)
+    lax.fori_loop(GROUP // BATCH, peers // BATCH - 1, add_batch, 0)
     add_terms(peers - BATCH, BATCH // 2)
     add_terms(peers - BATCH // 2, BATCH // 2)
 

time: 127 us -> 127 us (level)
  no operation moved by 1% of the time
where the time goes in v5:
time: 127 us
  Pallas kernels  126 us (99%)
    pallas_call x1, Pallas kernels, section(): pl.pallas_call(functools.partial(section_kernel, peers, inner, ring, wide...  123 us
    pallas_call x1, Pallas kernels, deliver(): pl.pallas_call(deliver_kernel, out_shape=tuple((jax.ShapeDtypeStruct(a.sh...  2.6 us

profile of v5, /device:TPU:1, one launch (start us, length us, event | category | flops | bytes accessed | tf_op | source)
XLA Modules:
  0.0 126.7 jit_solution(17230437493634880360)
XLA Ops:
  0.6 123.3 %section.1 = (bf16[96,8192]{1,0:T(8,128)(2,1)}, bf16[96,4096]{1,0:T(8,128)(2,1)}, bf16[4,24,96]{2,1,0:T(8,128)(2,1)}) custom-call(bf16[96,8192]{1,0:T(8,128)(2,1)} %act_hbm.1, bf16[96,8192]{1,0:T(8,128)(2,1)} %track_hbm.1, bf16[96,4096]{1,0:T(8,128)(2,1)} %coarse_hbm.1, bf16[4,96,768]{2,1,0:T(8,128)(2,1)} %weight_in_ref.1, s32[1,2048]{1,0:T(1,128)} %bitcast.5, ...), custom_call_target="tpu_custom_call" | custom-call | tf_op jit(solution)/shard_map/section/pallas_call | solution.py:511
  124.0 2.6 %deliver.1 = (bf16[96,8192]{1,0:T(8,128)(2,1)}, bf16[96,4096]{1,0:T(8,128)(2,1)}, bf16[4,24,96]{2,1,0:T(8,128)(2,1)}) custom-call(bf16[96,8192]{1,0:T(8,128)(2,1)} %get-tuple-element.9.skip_in, bf16[96,4096]{1,0:T(8,128)(2,1)} %get-tuple-element.10.coarse_in, bf16[4,24,96]{2,1,0:T(8,128)(2,1)} %get-tuple-element.11.weight_in), custom_call_target="tpu_custom_call" | custom-call | tf_op jit(solution)/shard_map/deliver/pallas_call | solution.py:579
